TPU v7x, 32 devices: a whole 2x2x4 slice. The times are simulated.
32 devices in a mesh: row: 8 (over z, y), col: 4 (over x, core).
Axes of the slice: x: 2, y: 2, z: 4, core: 2. Of those that a mesh axis runs over, the one named last changes fastest.
Arguments:
- hidden: bfloat16 [2048, 8192], P('row', 'col'), may hold values from -96 to 96
- norm_gain: bfloat16 [8192], P('col'), may hold values from 0.5 to 1.5
- w_query: bfloat16 [8192, 4096], P('row', 'col')
- w_key: bfloat16 [8192, 4096], P('row', 'col')
- w_value: bfloat16 [8192, 4096], P('row', 'col'), may hold values from -0.0625 to 0.0625
- w_out: bfloat16 [4096, 8192], P('row', 'col'), may hold values from -0.09375 to 0.09375
Outputs:
- context: bfloat16 [2048, 4096], P('row', 'col')
- layer_out: bfloat16 [2048, 8192], P('row', 'col')
All inputs are finite; a program needn't handle non-finite values.
Results may differ from a plain program's by a relative error of at most 0.04.
Values may be sent and summed in bfloat16 or wider, within the bound.
No kernel may reach another device: no remote copies, remote signals or barrier semaphores. Data moves between devices by JAX's collectives and lax.ppermute only.
A program may use at most 128 MiB of HBM per device.

v0:
```python
import math

import jax
import jax.numpy as jnp
from jax import lax
from jax.sharding import PartitionSpec as P

HD = 128


norm_epsilon = 1e-05


def rotary(values, positions):
    half = values.shape[-1] // 2
    freqs = jnp.exp(
        -math.log(10000.0) * 2.0 * jnp.arange(half, dtype=jnp.float32) / values.shape[-1]
    )
    angles = positions.astype(jnp.float32)[:, None] * freqs[None, :]
    cosine = jnp.cos(angles)[:, None, :]
    sine = jnp.sin(angles)[:, None, :]
    first = values[..., :half]
    second = values[..., half:]
    return jnp.concatenate(
        (first * cosine - second * sine, second * cosine + first * sine), axis=-1
    )


def attend(carry, keys, values, queries, query_positions, key_positions, scale):
    peak, total, weighted = carry
    scores = jnp.einsum("qhd,khd->hqk", queries, keys, preferred_element_type=jnp.float32) * scale
    allowed = key_positions[None, :] <= query_positions[:, None]
    scores = jnp.where(allowed[None, :, :], scores, -jnp.inf)
    new_peak = jnp.maximum(peak, jnp.max(scores, axis=2))
    probs = jnp.exp(scores - new_peak[:, :, None])
    total = jnp.sum(probs, axis=2)
    weighted = jnp.einsum(
        "hqk,khd->hqd", probs.astype(jnp.bfloat16), values, preferred_element_type=jnp.float32
    )
    return (new_peak, total, weighted)


def start_state(heads_here, count):
    return (
        jnp.full((heads_here, count), -1e30, jnp.float32),
        jnp.zeros((heads_here, count), jnp.float32),
        jnp.zeros((heads_here, count, HD), jnp.float32),
    )


def finish(carry, count, heads_here):
    peak, total, weighted = carry
    return (
        (weighted / total[:, :, None])
        .transpose(1, 0, 2)
        .reshape(count, heads_here * HD)
        .astype(jnp.bfloat16)
    )


def on_device(hidden, norm_gain, w_query, w_key, w_value, w_out):
    rows = hidden.shape[0]
    features = hidden.shape[1] * lax.axis_size("col")
    residual = hidden.astype(jnp.float32)
    squares = lax.psum(jnp.sum(residual * residual, axis=1), "col")
    scaled = (
        residual
        * lax.rsqrt(squares / features + norm_epsilon)[:, None]
        * norm_gain.astype(jnp.float32)[None, :]
    )
    normed = lax.all_gather(scaled.astype(jnp.bfloat16), "col", axis=1, tiled=True)
    spread = lax.all_to_all(normed, "row", split_axis=1, concat_axis=0, tiled=True)
    joined = jnp.concatenate((w_query, w_key, w_value), axis=1)
    segment = spread
    summed = lax.psum_scatter(
        jnp.dot(segment, joined, preferred_element_type=jnp.float32).astype(jnp.bfloat16),
        "row",
        scatter_dimension=0,
        tiled=True,
    ).astype(jnp.float32)
    proj_q, proj_k, proj_v = jnp.split(summed, 3, axis=1)
    heads_here = w_query.shape[1] // HD
    row_index = lax.axis_index("row")
    first_row = row_index * rows
    positions = first_row + jnp.arange(rows, dtype=jnp.int32)
    query = rotary(proj_q.reshape(rows, heads_here, HD), positions).astype(jnp.bfloat16)
    keys_here = (
        rotary(proj_k.reshape(rows, heads_here, HD), positions)
        .astype(jnp.bfloat16)
        .reshape(rows, heads_here * HD)
    )
    values_here = proj_v.astype(jnp.bfloat16)
    scale = 1.0 / math.sqrt(HD)
    initial = start_state(heads_here, rows)
    keys = lax.all_gather(keys_here, "row", axis=0, tiled=True).reshape(-1, heads_here, HD)
    values = lax.all_gather(values_here, "row", axis=0, tiled=True).reshape(-1, heads_here, HD)
    key_positions = jnp.arange(keys.shape[0], dtype=jnp.int32)
    folded = attend(initial, keys, values, query, positions, key_positions, scale)
    context = finish(folded, rows, heads_here)
    gathered_context = lax.all_gather(context, "col", axis=1, tiled=True)
    spread_context = lax.all_to_all(
        gathered_context, "row", split_axis=1, concat_axis=0, tiled=True
    )
    segment = spread_context
    attended = lax.psum_scatter(
        jnp.dot(segment, w_out, preferred_element_type=jnp.float32).astype(jnp.bfloat16),
        "row",
        scatter_dimension=0,
        tiled=True,
    ).astype(jnp.float32)
    layer_out = (residual + attended).astype(jnp.bfloat16)
    return (context, layer_out)


def solution(mesh):
    placed = (
        P("row", "col"),
        P("col"),
        P("row", "col"),
        P("row", "col"),
        P("row", "col"),
        P("row", "col"),
    )
    return jax.shard_map(
        on_device,
        mesh=mesh,
        in_specs=placed,
        out_specs=(P("row", "col"), P("row", "col")),
        check_vma=False,
    )
```

profile of v0, /device:TPU:0, one launch (start us, length us, event | category | flops | bytes accessed | tf_op | source)
XLA Modules:
  0.0 796.5 jit_solution(8590446164700002141)
XLA Ops:
  9.6 8.3 %psum.7 = f32[256]{0:T(256)S(1)} all-reduce(f32[256]{0:T(256)S(1)} %fusion.11), channel_id=1, replica_groups=mesh['row'=8,'col'=4] {'col'}, use_global_device_ids=true, to_apply=%region_1.0 | all-reduce | flops 256 | bytes 2048 | tf_op jit(solution)/shard_map/psum | solution.py:65
  17.9 2.5 fusion.13
  20.5 34.9 %all-gather.5.cloned.1.call-done = bf16[256,8192]{1,0:T(8,128)(2,1)} async-done(((bf16[256,2048]{1,0:T(8,128)(2,1)}), bf16[256,8192]{1,0:T(8,128)(2,1)}) %all-gather.5.cloned.1.call-update) | async-done | bytes 4194320 | tf_op jit(solution)/shard_map/all_gather | solution.py:71
  55.4 2.6 copy.51
  58.0 98.9 %all_to_all.38 = bf16[256,8,1024]{2,0,1:T(8,128)(2,1)S(1)} all-to-all(bf16[256,8,1024]{2,0,1:T(8,128)(2,1)S(1)} %bitcast.30), channel_id=1, replica_groups=mesh['row'=8,'col'=4] {'row'}, dimensions={1} | all-to-all | bytes 8388608 | tf_op jit(solution)/shard_map/all_to_all | solution.py:72
  156.9 18.5 %convolution_convert_fusion = bf16[2048,3072]{1,0:T(8,128)(2,1)} fusion(bf16[2048,1024]{1,0:T(8,128)(2,1)S(1)} %bitcast.37, bf16[1024,1024]{1,0:T(8,128)(2,1)} %param.10, bf16[1024,1024]{1,0:T(8,128)(2,1)} %param.9, bf16[1024,1024]{1,0:T(8,128)(2,1)} %param.8), kind=kOutput, calls=%fused_computation.5 | convolution fusion | flops 12910067712 | bytes 23068672 | tf_op jit(solution)/shard_map/dot_general | solution.py:76
  176.0 205.0 %reduce-scatter.3.cloned.1.call-done = bf16[256,3072]{1,0:T(8,128)(2,1)} async-done(((bf16[2048,3072]{1,0:T(8,128)(2,1)}), bf16[256,3072]{1,0:T(8,128)(2,1)}) %reduce-scatter.3.cloned.1.call-update) | async-done | bytes 1572880 | tf_op jit(solution)/shard_map/reduce_scatter | solution.py:75
  381.0 1.8 convert_element_type.52
  384.1 1.6 subtract_convert_fusion.1
  387.1 1.9 split.15
  389.6 71.7 %all-gather.7.cloned.1.call-done = bf16[2048,1024]{0,1:T(8,128)(2,1)} async-done(((bf16[256,1024]{0,1:T(8,128)(2,1)}), bf16[2048,1024]{0,1:T(8,128)(2,1)}) %all-gather.7.cloned.1.call-update) | async-done | bytes 4194320 | tf_op jit(solution)/shard_map/all_gather | solution.py:95
  461.3 5.8 fusion
  467.1 6.1 copy-done.1
  473.2 4.4 fusion.1
  477.6 57.9 %all-gather.9.cloned.1.call-done = bf16[2048,1024]{1,0:T(8,128)(2,1)} async-done(((bf16[256,1024]{1,0:T(8,128)(2,1)}), bf16[2048,1024]{1,0:T(8,128)(2,1)}) %all-gather.9.cloned.1.call-update) | async-done | bytes 4194320 | tf_op jit(solution)/shard_map/all_gather | solution.py:96
  535.5 6.5 copy.34
  542.0 10.3 %divide_convert_fusion = bf16[256,8,128]{0,2,1:T(8,128)(2,1)} fusion(bf16[2048,8,128]{0,2,1:T(8,128)(2,1)} %bitcast.36, f32[8,256,2048]{2,1,0:T(8,128)} %copy-done.1, f32[8,256]{1,0:T(8,128)S(1)} %broadcast_maximum_fusion, pred[256,2048]{1,0:T(8,128)(4,1)S(1)} %iota_compare_fusion, f32[256,8]{0,1:T(8,128)S(1)} %bitcast.43), kind=kOutput, calls=%fused_computation.26 | convolution fusion | flops 1091043328 | bytes 22036480 | tf_op jit(solution)/shard_map/hqk,khd->hqd/dot_general | solution.py:37
  552.3 20.9 %all-gather.11.cloned.1.call-done = bf16[256,4096]{0,1:T(8,128)(2,1)} async-done(((bf16[256,1024]{0,1:T(8,128)(2,1)}), bf16[256,4096]{0,1:T(8,128)(2,1)}) %all-gather.11.cloned.1.call-update) | async-done | bytes 2097168 | tf_op jit(solution)/shard_map/all_gather | solution.py:100
  573.3 54.2 %all_to_all.39 = bf16[256,8,512]{0,2,1:T(8,128)(2,1)} all-to-all(bf16[256,8,512]{0,2,1:T(8,128)(2,1)} %bitcast.38), channel_id=1, replica_groups=mesh['row'=8,'col'=4] {'row'}, dimensions={1} | all-to-all | bytes 4194304 | tf_op jit(solution)/shard_map/all_to_all | solution.py:101
  627.5 3.9 copy.31
  631.4 8.3 %convolution_convert_fusion.1 = bf16[2048,2048]{1,0:T(8,128)(2,1)} fusion(bf16[2048,512]{1,0:T(8,128)(2,1)} %bitcast.39, bf16[512,2048]{1,0:T(8,128)(2,1)S(1)} %copy-done), kind=kOutput, calls=%fused_computation.8 | convolution fusion | flops 4299161600 | bytes 12582912 | tf_op jit(solution)/shard_map/dot_general | solution.py:106
  639.8 2.1 copy.32
  641.9 145.2 %reduce-scatter.5.cloned.1.call-done = bf16[256,2048]{1,0:T(8,128)(2,1)} async-done(((bf16[2048,2048]{1,0:T(8,128)(2,1)}), bf16[256,2048]{1,0:T(8,128)(2,1)}) %reduce-scatter.5.cloned.1.call-update) | async-done | bytes 1048592 | tf_op jit(solution)/shard_map/reduce_scatter | solution.py:105
  787.1 2.6 fusion.14
  (32 shorter events, 6.4 us)
Async XLA Ops:
  7.2 624.3 %copy-start = (bf16[512,2048]{1,0:T(8,128)(2,1)S(1)}, bf16[512,2048]{1,0:T(8,128)(2,1)}, u32[]{:S(2)}) copy-start(bf16[512,2048]{1,0:T(8,128)(2,1)} %param.11) | copy-start | bytes 6291460
  7.2 48.2 %all-gather.5.cloned.1.call-start = ((), (), s32[]{:S(2)}) async-start(), calls=%async_computation.4 | async-start | bytes 5242880 | tf_op jit(solution)/shard_map/all_gather | solution.py:71
  20.4 360.5 %reduce-scatter.3.cloned.1.call-start = ((), (), s32[]{:S(2)}) async-start(), calls=%async_computation.5 | async-start | bytes 14155776 | tf_op jit(solution)/shard_map/reduce_scatter | solution.py:75
  175.4 285.9 %all-gather.7.cloned.1.call-start = ((), (), s32[]{:S(2)}) async-start(), calls=%async_computation.6 | async-start | bytes 4718592 | tf_op jit(solution)/shard_map/all_gather | solution.py:95
  387.0 148.5 %all-gather.9.cloned.1.call-start = ((), (), s32[]{:S(2)}) async-start(), calls=%async_computation.7 | async-start | bytes 4718592 | tf_op jit(solution)/shard_map/all_gather | solution.py:96
  389.0 184.3 %all-gather.11.cloned.1.call-start = ((), (), s32[]{:S(2)}) async-start(), calls=%async_computation.8 | async-start | bytes 2621440 | tf_op jit(solution)/shard_map/all_gather | solution.py:100
  467.1 6.1 copy-start.1
  552.3 234.8 %reduce-scatter.5.cloned.1.call-start = ((), (), s32[]{:S(2)}) async-start(), calls=%async_computation.9 | async-start | bytes 9437184 | tf_op jit(solution)/shard_map/reduce_scatter | solution.py:105
  639.7 147.3 %copy-start.2 = (bf16[256,2048]{1,0:T(8,128)(2,1)S(1)}, bf16[256,2048]{1,0:T(8,128)(2,1)}, u32[]{:S(2)}) copy-start(bf16[256,2048]{1,0:T(8,128)(2,1)} %param.6) | copy-start | bytes 3145732
Sparse Core Ops, SparseCore 0:
  20.6 34.7 all-gather.4
  175.5 205.4 reduce-scatter.2
  387.1 74.1 all-gather.6
  463.9 71.5 all-gather.8
  552.4 20.8 all-gather.10
  639.9 147.1 reduce-scatter.4
where the time goes:
time: 797 us
  waiting for transfers between devices  536 us (67%)
  blocking collectives  161 us (20%)
  matrix products  42.8 us (5%)
  local copies, waits for them, and re-layouts  25.4 us (3%)
  other arithmetic  16.4 us (2%)
  between operations  14.2 us (2%)
    reduce_scatter x1, waiting for transfers between devices, on_device(): lax.psum_scatter(jnp.dot(segment, joined, preferred_element_type=jnp.floa...  205 us
    reduce_scatter x1, waiting for transfers between devices, on_device(): lax.psum_scatter(jnp.dot(segment, w_out, preferred_element_type=jnp.float...  145 us
    all_to_all x1, blocking collectives, on_device(): lax.all_to_all(normed, 'row', split_axis=1, concat_axis=0, tiled=True)  98.9 us
    all_gather x1, waiting for transfers between devices, on_device(): lax.all_gather(keys_here, 'row', axis=0, tiled=True)  71.7 us
    all_gather x1, waiting for transfers between devices, on_device(): lax.all_gather(values_here, 'row', axis=0, tiled=True)  57.9 us
    all_to_all x1, blocking collectives, on_device(): lax.all_to_all(gathered_context, 'row', split_axis=1, concat_axis=0, tile...  54.2 us
    all_gather x1, waiting for transfers between devices, on_device(): lax.all_gather(scaled.astype(jnp.bfloat16), 'col', axis=1, tiled=True)  34.9 us
    all_gather x1, waiting for transfers between devices, on_device(): gathered_context = lax.all_gather(context, 'col', axis=1, tiled=True)  20.9 us
  transfers between devices with their start and end apart: 6, of which 6 were waited for; matrix products, arithmetic and copies ran while one was open for 2% of the time, Pallas kernels for 0%

commit v1 on v0

--- a/solution.py
+++ b/solution.py
@@ -3,6 +3,8 @@
 import jax
 import jax.numpy as jnp
 from jax import lax
+from jax.experimental import pallas as pl
+from jax.experimental.pallas import tpu as pltpu
 from jax.sharding import PartitionSpec as P
 
 HD = 128
@@ -58,7 +60,7 @@
     )
 
 
-def on_device(hidden, norm_gain, w_query, w_key, w_value, w_out):
+def on_device_any(hidden, norm_gain, w_query, w_key, w_value, w_out):
     rows = hidden.shape[0]
     features = hidden.shape[1] * lax.axis_size("col")
     residual = hidden.astype(jnp.float32)
@@ -71,9 +73,8 @@
     normed = lax.all_gather(scaled.astype(jnp.bfloat16), "col", axis=1, tiled=True)
     spread = lax.all_to_all(normed, "row", split_axis=1, concat_axis=0, tiled=True)
     joined = jnp.concatenate((w_query, w_key, w_value), axis=1)
-    segment = spread
     summed = lax.psum_scatter(
-        jnp.dot(segment, joined, preferred_element_type=jnp.float32).astype(jnp.bfloat16),
+        jnp.dot(spread, joined, preferred_element_type=jnp.float32).astype(jnp.bfloat16),
         "row",
         scatter_dimension=0,
         tiled=True,
@@ -101,9 +102,8 @@
     spread_context = lax.all_to_all(
         gathered_context, "row", split_axis=1, concat_axis=0, tiled=True
     )
-    segment = spread_context
     attended = lax.psum_scatter(
-        jnp.dot(segment, w_out, preferred_element_type=jnp.float32).astype(jnp.bfloat16),
+        jnp.dot(spread_context, w_out, preferred_element_type=jnp.float32).astype(jnp.bfloat16),
         "row",
         scatter_dimension=0,
         tiled=True,
@@ -112,6 +112,202 @@
     return (context, layer_out)
 
 
+def attention_kernel(block, q_ref, k_ref, v_ref, inv_ref, cos_ref, sin_ref, out_ref, keys, values):
+    length = q_ref.shape[0]
+    half = HD // 2
+    factor = math.log2(math.e) / math.sqrt(HD)
+
+    def turned(ref, at):
+        raw = ref[at, :] * inv_ref[at, :]
+        return (raw * cos_ref[at, :] + pltpu.roll(raw, half, 1) * sin_ref[at, :]).astype(
+            jnp.bfloat16
+        )
+
+    for start in range(0, length, block):
+        at = pl.ds(start, block)
+        stop = start + block
+        keys[at, :] = turned(k_ref, at)
+        values[at, :] = (v_ref[at, :] * inv_ref[at, :]).astype(jnp.bfloat16)
+        query = turned(q_ref, at)
+        scores = lax.dot_general(
+            query,
+            keys[0:stop, :],
+            (((1,), (1,)), ((), ())),
+            preferred_element_type=jnp.float32,
+        )
+        row = lax.broadcasted_iota(jnp.int32, scores.shape, 0) + start
+        column = lax.broadcasted_iota(jnp.int32, scores.shape, 1)
+        scores = jnp.where(column <= row, scores, -jnp.inf)
+        peak = jnp.max(scores, axis=1, keepdims=True)
+        probs = jnp.exp2((scores - peak) * factor)
+        total = jnp.sum(probs, axis=1, keepdims=True)
+        weighted = jnp.dot(
+            probs.astype(jnp.bfloat16), values[0:stop, :], preferred_element_type=jnp.float32
+        )
+        out_ref[at, :] = (weighted / total).astype(jnp.bfloat16)
+
+
+def attention(query, key, value, inverse):
+    length = query.shape[0]
+    half = HD // 2
+    freqs = jnp.exp(-math.log(10000.0) * 2.0 * jnp.arange(half, dtype=jnp.float32) / HD)
+    angles = jnp.arange(length, dtype=jnp.int32).astype(jnp.float32)[:, None] * freqs[None, :]
+    cosine = jnp.cos(angles)
+    sine = jnp.sin(angles)
+    whole = pl.BlockSpec(memory_space=pltpu.VMEM)
+    return pl.pallas_call(
+        lambda *refs: attention_kernel(min(256, length), *refs),
+        out_shape=jax.ShapeDtypeStruct((length, HD), jnp.bfloat16),
+        in_specs=[whole] * 6,
+        out_specs=whole,
+        scratch_shapes=[pltpu.VMEM((length, HD), jnp.bfloat16)] * 2,
+        compiler_params=pltpu.CompilerParams(vmem_limit_bytes=48 * 1024 * 1024),
+        cost_estimate=pl.CostEstimate(
+            flops=2 * length * length * HD,
+            bytes_accessed=16 * length * HD,
+            transcendentals=length * length // 2,
+        ),
+    )(
+        query,
+        key,
+        value,
+        inverse,
+        jnp.concatenate((cosine, cosine), axis=1),
+        jnp.concatenate((-sine, sine), axis=1),
+    )
+
+
+def on_device_paired(hidden, norm_gain, w_query, w_key, w_value, w_out):
+    rows, cols = lax.axis_size("row"), lax.axis_size("col")
+    tokens = hidden.shape[0]
+    length = tokens * rows
+    row, col = lax.axis_index("row"), lax.axis_index("col")
+    bits = {
+        "y": (row & 1, "row", 1),
+        "zl": ((row >> 1) & 1, "row", 2),
+        "zh": ((row >> 2) & 1, "row", 4),
+        "core": (col & 1, "col", 1),
+        "x": ((col >> 1) & 1, "col", 2),
+    }
+
+    def swap(values, name):
+        _, axis, step = bits[name]
+        count = rows if axis == "row" else cols
+        return lax.ppermute(values, axis, [(i, i ^ step) for i in range(count)])
+
+    def parts(values, axis, name):
+        bit = bits[name][0]
+        keep = lax.dynamic_index_in_dim(values, bit, axis, keepdims=False)
+        send = lax.dynamic_index_in_dim(values, 1 - bit, axis, keepdims=False)
+        return keep, send
+
+    def ordered(mine, other, name):
+        low = bits[name][0] == 0
+        return jnp.where(low, mine, other), jnp.where(low, other, mine)
+
+    def joined(mine, other, name):
+        return jnp.stack(ordered(mine, other, name))
+
+    def deepened(weight):
+        depth = weight.shape[0]
+        split = weight.reshape(depth, 2, 2, 2 * HD)
+        keep, send = parts(split, 2, "zl")
+        return ordered(
+            keep.reshape(depth, 4 * HD), swap(send, "zl").reshape(depth, 4 * HD), "zl"
+        )
+
+    weights = [deepened(w) for w in (w_value, w_key, w_query)]
+    out_depth, out_width = w_out.shape
+    keep, send = parts(w_out.reshape(out_depth, 2, out_width // 2), 1, "zl")
+    weight_out = jnp.concatenate(ordered(keep, swap(send, "zl"), "zl"), axis=0)
+
+    residual = hidden.astype(jnp.float32)
+    squares = lax.all_gather(jnp.sum(residual * residual, axis=1), ("row", "col"))
+    mean = jnp.sum(squares.reshape(rows, cols, tokens), axis=1) / (hidden.shape[1] * cols)
+    inverse = lax.rsqrt(mean + norm_epsilon).reshape(length, 1)
+
+    gained = (residual * norm_gain.astype(jnp.float32)[None, :]).astype(jnp.bfloat16)
+    width = hidden.shape[1] // 2
+    chunks = 4
+    step = tokens // chunks
+    collected = ([], [], [])
+    for chunk in range(chunks):
+        block = gained[chunk * step : (chunk + 1) * step].reshape(step, 2, width)
+        keep, send = parts(block, 1, "y")
+        block = joined(keep, swap(send, "y"), "y").reshape(2, 2, step // 2, width)
+        keep, send = parts(block, 1, "x")
+        block = joined(keep, swap(send, "x"), "x")
+        keep, send = parts(block, 0, "zh")
+        block = joined(keep, swap(send, "zh"), "zh")
+        block = joined(block, swap(block, "zl"), "zl")
+        block = joined(block, swap(block, "x"), "x").reshape(step * rows, width)
+        first, second = ordered(block, swap(block, "core"), "core")
+        for (low, high), results in zip(weights, collected):
+            part = (
+                jnp.dot(first, low, preferred_element_type=jnp.float32)
+                + jnp.dot(second, high, preferred_element_type=jnp.float32)
+            ).astype(jnp.bfloat16)
+            keep, send = parts(part.reshape(step * rows, 2, 2 * HD), 1, "y")
+            part = (keep.astype(jnp.float32) + swap(send, "y").astype(jnp.float32)).astype(
+                jnp.bfloat16
+            )
+            keep, send = parts(part.reshape(step * rows, 2, HD), 1, "zh")
+            part = keep.astype(jnp.float32) + swap(send, "zh").astype(jnp.float32)
+            results.append(part.reshape(2, 2, 2, 2, step // 2, HD))
+
+    def in_order(results):
+        return jnp.stack(results).transpose(3, 2, 4, 0, 1, 5, 6).reshape(length, HD)
+
+    value, key, query = (in_order(results) for results in collected)
+    context = attention(query, key, value, inverse)
+
+    blocks = context.reshape(rows, tokens, HD)
+    home = jnp.zeros((tokens, rows, HD), jnp.bfloat16)
+    for mask in range(rows):
+        peer = row ^ mask
+        block = lax.dynamic_index_in_dim(blocks, peer, 0, keepdims=False)
+        if mask:
+            block = lax.ppermute(block, "row", [(i, i ^ mask) for i in range(rows)])
+        head = ((peer & 1) << 2) | (peer & 2) | (peer >> 2)
+        home = lax.dynamic_update_slice_in_dim(home, block[:, None, :], head, 1)
+    context_out = home.reshape(tokens, rows * HD)
+
+    pieces = []
+    for chunk in range(chunks):
+        block = blocks[:, chunk * step : (chunk + 1) * step].reshape(rows, 2, step // 2, HD)
+        keep, send = parts(block, 1, "x")
+        block = joined(keep, swap(send, "x"), "x")
+        keep, send = parts(block, 0, "zh")
+        block = joined(keep, swap(send, "zh"), "zh")
+        block = joined(block, swap(block, "zl"), "zl")
+        block = joined(block, swap(block, "x"), "x")
+        block = joined(block, swap(block, "core"), "core")
+        block = block.transpose(4, 1, 5, 0, 2, 3, 6).reshape(rows * step, 8 * HD)
+        part = jnp.dot(block, weight_out, preferred_element_type=jnp.float32).astype(jnp.bfloat16)
+        part = part.reshape(4, 2, step, out_width // 2)
+        keep, send = parts(part, 1, "y")
+        part = (keep.astype(jnp.float32) + swap(send, "y").astype(jnp.float32)).astype(
+            jnp.bfloat16
+        )
+        keep, send = parts(part.reshape(2, 2, step, out_width // 2), 0, "zh")
+        part = (keep.astype(jnp.float32) + swap(send, "zh").astype(jnp.float32)).astype(
+            jnp.bfloat16
+        )
+        keep, send = parts(part, 0, "zl")
+        pieces.append(jnp.concatenate(ordered(keep, swap(send, "zl"), "zl"), axis=1))
+    attended = jnp.concatenate(pieces, axis=0).astype(jnp.float32)
+    layer_out = (residual + attended).astype(jnp.bfloat16)
+    return (context_out, layer_out)
+
+
+def on_device(hidden, norm_gain, w_query, w_key, w_value, w_out):
+    rows, cols = lax.axis_size("row"), lax.axis_size("col")
+    heads_here = w_query.shape[1] // HD
+    paired = rows == 2**3 and cols == 2**2 and heads_here == rows and hidden.shape[0] % 64 == 0
+    plan = on_device_paired if paired else on_device_any
+    return plan(hidden, norm_gain, w_query, w_key, w_value, w_out)
+
+
 def solution(mesh):
     placed = (
         P("row", "col"),

time: 797 us -> 562 us (0.71)
  waiting for transfers between devices: 536 us -> 207 us
  blocking collectives: 161 us -> 41 us
  starting transfers between devices: 0.43 us -> 111 us
  local copies, waits for them, and re-layouts: 25.4 us -> 104 us
  other arithmetic: 16.4 us -> 52.4 us
  matrix products: 42.8 us -> 29.1 us
  between operations: 14.2 us -> 2.99 us
    reduce_scatter x2 -> x0, waiting for transfers between devices: 350 us -> none  [the longest x1 205 us: on_device(): lax.psum_scatter(jnp.dot(segment, joined, preferred_element_type=jnp.floa...]
    ppermute x0 -> x91, waiting for transfers between devices: none -> 207 us  [the longest x84 207 us: swap(): return lax.ppermute(values, axis, [(i, i ^ step) for i in range(count)])]
    all_gather x4 -> x0, waiting for transfers between devices: 185 us -> none  [the longest x1 71.7 us: on_device(): lax.all_gather(keys_here, 'row', axis=0, tiled=True)]
    all_to_all x2 -> x0, blocking collectives: 153 us -> none  [the longest x1 98.9 us: on_device(): lax.all_to_all(normed, 'row', split_axis=1, concat_axis=0, tiled=True)]
    ppermute x0 -> x91, starting transfers between devices: none -> 111 us  [the longest x84 100 us: swap(): return lax.ppermute(values, axis, [(i, i ^ step) for i in range(count)])]
    all_gather x0 -> x1, blocking collectives: none -> 41 us  [on_device_paired(): lax.all_gather(jnp.sum(residual * residual, axis=1), ('row', 'col'))]
    dynamic_update_slice x0 -> x8, local copies, waits for them, and re-layouts: none -> 23 us  [on_device_paired(): home = lax.dynamic_update_slice_in_dim(home, block[:, None, :], head, 1)]
    dynamic_slice x0 -> x12, local copies, waits for them, and re-layouts: none -> 21.2 us  [the longest x8 12.9 us: parts(): keep = lax.dynamic_index_in_dim(values, bit, axis, keepdims=False)]
  transfers between devices with their start and end apart: 6 -> 91, of which waited for: 6 -> 50; matrix products, arithmetic and copies ran while one was open for 2% -> 30% of each run, Pallas kernels for 0% -> 0%
where the time goes in v1:
time: 562 us; the launch traced here: 556 us
  waiting for transfers between devices  207 us (37%)
  starting transfers between devices  111 us (20%)
  local copies, waits for them, and re-layouts  104 us (19%)
  other arithmetic  52.4 us (9%)
  blocking collectives  41 us (7%)
  matrix products  29.1 us (5%)
  Pallas kernels  7.23 us (1%)
    ppermute x84, waiting for transfers between devices, swap(): return lax.ppermute(values, axis, [(i, i ^ step) for i in range(count)])  207 us
    ppermute x84, starting transfers between devices, swap(): return lax.ppermute(values, axis, [(i, i ^ step) for i in range(count)])  100 us
    all_gather x1, blocking collectives, on_device_paired(): lax.all_gather(jnp.sum(residual * residual, axis=1), ('row', 'col'))  41 us
    dynamic_update_slice x8, local copies, waits for them, and re-layouts, on_device_paired(): home = lax.dynamic_update_slice_in_dim(home, block[:, None, :], head, 1)  23 us
    unnamed x99, local copies, waits for them, and re-layouts  20.2 us
    another operation x60, other arithmetic, joined(): return jnp.stack(ordered(mine, other, name))  14.6 us
    dynamic_slice x8, local copies, waits for them, and re-layouts, parts(): keep = lax.dynamic_index_in_dim(values, bit, axis, keepdims=False)  12.9 us
    dot_general x4, matrix products, on_device_paired(): jnp.dot(block, weight_out, preferred_element_type=jnp.float32)  11.2 us
  transfers between devices with their start and end apart: 91, of which 50 were waited for; matrix products, arithmetic and copies ran while one was open for 30% of the time, Pallas kernels for 0%

profile of v1, /device:TPU:0, one launch (start us, length us, event | category | flops | bytes accessed | tf_op | source)
XLA Modules:
  0.0 555.8 jit_solution(11431657188842772606)
XLA Ops:
  10.5 4.0 copy.99
  38.9 41.0 %all-gather.1 = f32[32,1,256]{2,1,0:T(1,128)S(1)} all-gather(f32[1,1,256]{2,1,0:T(1,128)S(1)} %bitcast.807), channel_id=2, replica_groups=mesh['row'=8,'col'=4] {'row','col'}, dimensions={0}, use_global_device_ids=true | all-gather | bytes 33792 | tf_op jit(solution)/shard_map/all_gather | solution.py:225
  80.3 4.0 copy.125
  84.3 3.7 fusion.35
  115.6 29.1 %collective-permute-done.2 = bf16[2,32,1024]{2,1,0:T(8,128)(2,1)S(1)} collective-permute-done((bf16[2,32,1024]{2,1,0:T(8,128)(2,1)S(1)}, bf16[2,32,1024]{2,1,0:T(8,128)(2,1)S(1)}, u32[]{:S(2)}, u32[]{:S(2)}) %collective-permute-start.2) | collective-permute-done | bytes 131104 | tf_op jit(solution)/shard_map/ppermute | solution.py:196
  157.8 3.8 collective-permute-done.3
  163.1 4.1 collective-permute-done.12
  168.7 4.1 collective-permute-done.20
  176.9 23.0 %collective-permute-done.28 = bf16[2,2,32,1024]{3,2,1,0:T(8,128)(2,1)S(1)} collective-permute-done((bf16[2,2,32,1024]{3,2,1,0:T(8,128)(2,1)S(1)}, bf16[2,2,32,1024]{3,2,1,0:T(8,128)(2,1)S(1)}, u32[]{:S(2)}, u32[]{:S(2)}) %collective-permute-start.28) | collective-permute-done | bytes 262176 | tf_op jit(solution)/shard_map/ppermute | solution.py:196
  221.8 4.6 collective-permute-done.13
  227.7 9.9 %collective-permute-done.21 = bf16[2,2,2,32,1024]{4,3,2,1,0:T(8,128)(2,1)} collective-permute-done((bf16[2,2,2,32,1024]{4,3,2,1,0:T(8,128)(2,1)}, bf16[2,2,2,32,1024]{4,3,2,1,0:T(8,128)(2,1)}, u32[]{:S(2)}, u32[]{:S(2)}) %collective-permute-start.21) | collective-permute-done | bytes 524320 | tf_op jit(solution)/shard_map/ppermute | solution.py:196
  238.9 8.0 %collective-permute-done.29 = bf16[2,2,2,32,1024]{4,3,2,1,0:T(8,128)(2,1)} collective-permute-done((bf16[2,2,2,32,1024]{4,3,2,1,0:T(8,128)(2,1)}, bf16[2,2,2,32,1024]{4,3,2,1,0:T(8,128)(2,1)}, u32[]{:S(2)}, u32[]{:S(2)}) %collective-permute-start.29) | collective-permute-done | bytes 524320 | tf_op jit(solution)/shard_map/ppermute | solution.py:196
  282.0 3.6 collective-permute-done.49
  304.5 3.6 collective-permute-done.40
  343.4 8.2 %collective-permute-done.35 = bf16[512,128]{0,1:T(8,128)(2,1)S(1)} collective-permute-done((bf16[512,128]{0,1:T(8,128)(2,1)}, bf16[512,128]{0,1:T(8,128)(2,1)S(1)}, u32[]{:S(2)}, u32[]{:S(2)}) %collective-permute-start.35) | collective-permute-done | bytes 131104 | tf_op jit(solution)/shard_map/ppermute | solution.py:196
  362.0 3.8 collective-permute-done.41
  382.4 7.2 %shard_map.77 = bf16[2048,128]{1,0:T(8,128)(2,1)S(1)} custom-call(f32[2048,128]{1,0:T(8,128)S(1)} %bitcast.685, f32[2048,128]{1,0:T(8,128)S(1)} %bitcast.684, f32[2048,128]{1,0:T(8,128)S(1)} %bitcast.683, f32[2048,1]{1,0:T(8,128)S(1)} %bitcast.682, f32[2048,128]{1,0:T(8,128)S(1)} %get-tuple-element.145.refs_4_, f32[2048,128]{1,0:T(8,128)} %get-tuple-element.146.refs_5_), custom_call_target="tpu_custom_call" | custom-call | flops 1073741824 | bytes 4194304 | tf_op jit(solution)/shard_map/pallas_call | solution.py:158
  413.5 5.3 collective-permute-start.84
  500.9 6.9 %collective-permute-done.80 = bf16[4,64,1024]{2,1,0:T(8,128)(2,1)} collective-permute-done((bf16[4,64,1024]{2,1,0:T(8,128)(2,1)}, bf16[4,64,1024]{2,1,0:T(8,128)(2,1)}, u32[]{:S(2)}, u32[]{:S(2)}) %collective-permute-start.80) | collective-permute-done | bytes 524320 | tf_op jit(solution)/shard_map/ppermute | solution.py:196
  510.0 8.5 %collective-permute-done.88 = bf16[4,64,1024]{2,1,0:T(8,128)(2,1)S(1)} collective-permute-done((bf16[4,64,1024]{2,1,0:T(8,128)(2,1)S(1)}, bf16[4,64,1024]{2,1,0:T(8,128)(2,1)S(1)}, u32[]{:S(2)}, u32[]{:S(2)}) %collective-permute-start.88) | collective-permute-done | bytes 524320 | tf_op jit(solution)/shard_map/ppermute | solution.py:196
  519.8 6.8 %collective-permute-done.65 = bf16[2,64,1024]{2,1,0:T(8,128)(2,1)S(1)} collective-permute-done((bf16[2,64,1024]{2,1,0:T(8,128)(2,1)S(1)}, bf16[2,64,1024]{2,1,0:T(8,128)(2,1)S(1)}, u32[]{:S(2)}, u32[]{:S(2)}) %collective-permute-start.65) | collective-permute-done | bytes 262176 | tf_op jit(solution)/shard_map/ppermute | solution.py:196
  526.7 6.6 %collective-permute-done.73 = bf16[2,64,1024]{2,1,0:T(8,128)(2,1)S(1)} collective-permute-done((bf16[2,64,1024]{2,1,0:T(8,128)(2,1)S(1)}, bf16[2,64,1024]{2,1,0:T(8,128)(2,1)S(1)}, u32[]{:S(2)}, u32[]{:S(2)}) %collective-permute-start.73) | collective-permute-done | bytes 262176 | tf_op jit(solution)/shard_map/ppermute | solution.py:196
  533.5 5.4 collective-permute-done.81
  539.1 5.4 collective-permute-done.89
  (527 shorter events, 342.4 us)
Async XLA Ops:
  4.6 91.0 %collective-permute-start = (bf16[64,1024]{1,0:T(8,128)(2,1)S(1)}, bf16[64,1024]{1,0:T(8,128)(2,1)}, u32[]{:S(2)}, u32[]{:S(2)}) collective-permute-start(bf16[64,1024]{1,0:T(8,128)(2,1)S(1)} %bitcast.798), channel_id=1, source_target_pairs={{0,4},{4,0},{8,12},{12,8},{16,20},{20,16},{24,28},{28,24},{1,5},{5... | collective-permute-start | bytes 393224 | tf_op jit(solution)/shard_map/ppermute | solution.py:196
  20.3 182.6 %collective-permute-start.42 = (bf16[1024,2,256]{2,0,1:T(8,128)(2,1)}, bf16[1024,2,256]{2,0,1:T(8,128)(2,1)}, u32[]{:S(2)}, u32[]{:S(2)}) collective-permute-start(bf16[1024,2,256]{2,0,1:T(8,128)(2,1)} %bitcast.130), channel_id=1, source_target_pairs={{0,8},{4,12},{8,0},{12,4},{16,24},{20,28},{24,16},{28,20},{1,9},{5... | collective-permute-start | bytes 3145736 | tf_op jit(solution)/shard_map/ppermute | solution.py:196
  24.0 72.7 %collective-permute-start.9 = (bf16[64,1024]{1,0:T(8,128)(2,1)}, bf16[64,1024]{1,0:T(8,128)(2,1)}, u32[]{:S(2)}, u32[]{:S(2)}) collective-permute-start(bf16[64,1024]{1,0:T(8,128)(2,1)} %bitcast.678), channel_id=1, source_target_pairs={{0,4},{4,0},{8,12},{12,8},{16,20},{20,16},{24,28},{28,24},{1,5},{5... | collective-permute-start | bytes 393224 | tf_op jit(solution)/shard_map/ppermute | solution.py:196
  26.6 73.2 %collective-permute-start.17 = (bf16[64,1024]{1,0:T(8,128)(2,1)}, bf16[64,1024]{1,0:T(8,128)(2,1)}, u32[]{:S(2)}, u32[]{:S(2)}) collective-permute-start(bf16[64,1024]{1,0:T(8,128)(2,1)} %bitcast.677), channel_id=1, source_target_pairs={{0,4},{4,0},{8,12},{12,8},{16,20},{20,16},{24,28},{28,24},{1,5},{5... | collective-permute-start | bytes 393224 | tf_op jit(solution)/shard_map/ppermute | solution.py:196
  30.3 70.8 %collective-permute-start.25 = (bf16[64,1024]{1,0:T(8,128)(2,1)}, bf16[64,1024]{1,0:T(8,128)(2,1)}, u32[]{:S(2)}, u32[]{:S(2)}) collective-permute-start(bf16[64,1024]{1,0:T(8,128)(2,1)} %bitcast.676), channel_id=1, source_target_pairs={{0,4},{4,0},{8,12},{12,8},{16,20},{20,16},{24,28},{28,24},{1,5},{5... | collective-permute-start | bytes 393224 | tf_op jit(solution)/shard_map/ppermute | solution.py:196
  95.7 110.2 %collective-permute-start.33 = (bf16[1024,2,256]{2,0,1:T(8,128)(2,1)}, bf16[1024,2,256]{2,0,1:T(8,128)(2,1)}, u32[]{:S(2)}, u32[]{:S(2)}) collective-permute-start(bf16[1024,2,256]{2,0,1:T(8,128)(2,1)} %bitcast.720), channel_id=1, source_target_pairs={{0,8},{4,12},{8,0},{12,4},{16,24},{20,28},{24,16},{28,20},{1,9},{5... | collective-permute-start | bytes 3145736 | tf_op jit(solution)/shard_map/ppermute | solution.py:196
  96.7 112.8 %collective-permute-start.6 = (bf16[1024,2,256]{2,0,1:T(8,128)(2,1)}, bf16[1024,2,256]{2,0,1:T(8,128)(2,1)}, u32[]{:S(2)}, u32[]{:S(2)}) collective-permute-start(bf16[1024,2,256]{2,0,1:T(8,128)(2,1)} %bitcast.719), channel_id=1, source_target_pairs={{0,8},{4,12},{8,0},{12,4},{16,24},{20,28},{24,16},{28,20},{1,9},{5... | collective-permute-start | bytes 3145736 | tf_op jit(solution)/shard_map/ppermute | solution.py:196
  112.3 32.4 %collective-permute-start.2 = (bf16[2,32,1024]{2,1,0:T(8,128)(2,1)S(1)}, bf16[2,32,1024]{2,1,0:T(8,128)(2,1)S(1)}, u32[]{:S(2)}, u32[]{:S(2)}) collective-permute-start(bf16[2,32,1024]{2,1,0:T(8,128)(2,1)S(1)} %fusion.61), channel_id=1, source_target_pairs={{0,16},{4,20},{8,24},{12,28},{16,0},{20,4},{24,8},{28,12},{1,17},{... | collective-permute-start | bytes 393224 | tf_op jit(solution)/shard_map/ppermute | solution.py:196
  114.0 34.2 %collective-permute-start.11 = (bf16[2,32,1024]{2,1,0:T(8,128)(2,1)S(1)}, bf16[2,32,1024]{2,1,0:T(8,128)(2,1)S(1)}, u32[]{:S(2)}, u32[]{:S(2)}) collective-permute-start(bf16[2,32,1024]{2,1,0:T(8,128)(2,1)S(1)} %fusion.53), channel_id=1, source_target_pairs={{0,16},{4,20},{8,24},{12,28},{16,0},{20,4},{24,8},{28,12},{1,17},{... | collective-permute-start | bytes 393224 | tf_op jit(solution)/shard_map/ppermute | solution.py:196
  167.2 49.5 %collective-permute-start.63 = (bf16[512,1024]{1,0:T(8,128)(2,1)}, bf16[512,1024]{1,0:T(8,128)(2,1)}, u32[]{:S(2)}, u32[]{:S(2)}) collective-permute-start(bf16[512,1024]{1,0:T(8,128)(2,1)} %bitcast.197), channel_id=1, source_target_pairs={{0,8},{4,12},{8,0},{12,4},{16,24},{20,28},{24,16},{28,20},{1,9},{5... | collective-permute-start | bytes 3145736 | tf_op jit(solution)/shard_map/ppermute | solution.py:196
  205.9 31.7 %collective-permute-start.21 = (bf16[2,2,2,32,1024]{4,3,2,1,0:T(8,128)(2,1)}, bf16[2,2,2,32,1024]{4,3,2,1,0:T(8,128)(2,1)}, u32[]{:S(2)}, u32[]{:S(2)}) collective-permute-start(bf16[2,2,2,32,1024]{4,3,2,1,0:T(8,128)(2,1)} %pad_maximum_fusion.9), channel_id=1, source_target_pairs={{0,2},{1,3},{2,0},{3,1},{4,6},{5,7},{6,4},{7,5},{8,10},{9,11},{10,... | collective-permute-start | bytes 1572872 | tf_op jit(solution)/shard_map/ppermute | solution.py:196
  209.6 37.3 %collective-permute-start.29 = (bf16[2,2,2,32,1024]{4,3,2,1,0:T(8,128)(2,1)}, bf16[2,2,2,32,1024]{4,3,2,1,0:T(8,128)(2,1)}, u32[]{:S(2)}, u32[]{:S(2)}) collective-permute-start(bf16[2,2,2,32,1024]{4,3,2,1,0:T(8,128)(2,1)} %pad_maximum_fusion.10), channel_id=1, source_target_pairs={{0,2},{1,3},{2,0},{3,1},{4,6},{5,7},{6,4},{7,5},{8,10},{9,11},{10,... | collective-permute-start | bytes 1572872 | tf_op jit(solution)/shard_map/ppermute | solution.py:196
  280.0 28.1 %collective-permute-start.40 = (bf16[512,256]{0,1:T(8,128)(2,1)S(1)}, bf16[512,256]{0,1:T(8,128)(2,1)S(1)}, u32[]{:S(2)}, u32[]{:S(2)}) collective-permute-start(bf16[512,256]{0,1:T(8,128)(2,1)S(1)} %dynamic-slice_bitcast_fusion.12), channel_id=1, source_target_pairs={{0,4},{4,0},{8,12},{12,8},{16,20},{20,16},{24,28},{28,24},{1,5},{5... | collective-permute-start | bytes 786440 | tf_op jit(solution)/shard_map/ppermute | solution.py:196
  285.6 28.1 %collective-permute-start.7 = (bf16[512,256]{0,1:T(8,128)(2,1)S(1)}, bf16[512,256]{0,1:T(8,128)(2,1)S(1)}, u32[]{:S(2)}, u32[]{:S(2)}) collective-permute-start(bf16[512,256]{0,1:T(8,128)(2,1)S(1)} %dynamic-slice_bitcast_fusion.19), channel_id=1, source_target_pairs={{0,4},{4,0},{8,12},{12,8},{16,20},{20,16},{24,28},{28,24},{1,5},{5... | collective-permute-start | bytes 786440 | tf_op jit(solution)/shard_map/ppermute | solution.py:196
  291.2 28.1 %collective-permute-start.15 = (bf16[512,256]{0,1:T(8,128)(2,1)S(1)}, bf16[512,256]{0,1:T(8,128)(2,1)S(1)}, u32[]{:S(2)}, u32[]{:S(2)}) collective-permute-start(bf16[512,256]{0,1:T(8,128)(2,1)S(1)} %dynamic-slice_bitcast_fusion.18), channel_id=1, source_target_pairs={{0,4},{4,0},{8,12},{12,8},{16,20},{20,16},{24,28},{28,24},{1,5},{5... | collective-permute-start | bytes 786440 | tf_op jit(solution)/shard_map/ppermute | solution.py:196
  296.8 28.1 %collective-permute-start.23 = (bf16[512,256]{0,1:T(8,128)(2,1)S(1)}, bf16[512,256]{0,1:T(8,128)(2,1)S(1)}, u32[]{:S(2)}, u32[]{:S(2)}) collective-permute-start(bf16[512,256]{0,1:T(8,128)(2,1)S(1)} %dynamic-slice_bitcast_fusion.17), channel_id=1, source_target_pairs={{0,4},{4,0},{8,12},{12,8},{16,20},{20,16},{24,28},{28,24},{1,5},{5... | collective-permute-start | bytes 786440 | tf_op jit(solution)/shard_map/ppermute | solution.py:196
  340.1 29.8 %collective-permute-start.8 = (bf16[512,128]{0,1:T(8,128)(2,1)}, bf16[512,128]{0,1:T(8,128)(2,1)}, u32[]{:S(2)}, u32[]{:S(2)}) collective-permute-start(bf16[512,128]{0,1:T(8,128)(2,1)} %dynamic-slice_bitcast_fusion.35), channel_id=1, source_target_pairs={{0,16},{4,20},{8,24},{12,28},{16,0},{20,4},{24,8},{28,12},{1,17},{... | collective-permute-start | bytes 393224 | tf_op jit(solution)/shard_map/ppermute | solution.py:196
  409.6 30.6 %collective-permute-start.59 = (bf16[8,32,128]{2,1,0:T(8,128)(2,1)S(1)}, bf16[8,32,128]{2,1,0:T(8,128)(2,1)S(1)}, u32[]{:S(2)}, u32[]{:S(2)}) collective-permute-start(bf16[8,32,128]{2,1,0:T(8,128)(2,1)S(1)} %fusion.81), channel_id=1, source_target_pairs={{0,16},{4,20},{8,24},{12,28},{16,0},{20,4},{24,8},{28,12},{1,17},{... | collective-permute-start | bytes 196616 | tf_op jit(solution)/shard_map/ppermute | solution.py:196
  410.3 31.4 %collective-permute-start.68 = (bf16[8,32,128]{2,1,0:T(8,128)(2,1)S(1)}, bf16[8,32,128]{2,1,0:T(8,128)(2,1)S(1)}, u32[]{:S(2)}, u32[]{:S(2)}) collective-permute-start(bf16[8,32,128]{2,1,0:T(8,128)(2,1)S(1)} %fusion.77), channel_id=1, source_target_pairs={{0,16},{4,20},{8,24},{12,28},{16,0},{20,4},{24,8},{28,12},{1,17},{... | collective-permute-start | bytes 196616 | tf_op jit(solution)/shard_map/ppermute | solution.py:196
  412.8 29.6 %collective-permute-start.76 = (bf16[8,32,128]{2,1,0:T(8,128)(2,1)S(1)}, bf16[8,32,128]{2,1,0:T(8,128)(2,1)S(1)}, u32[]{:S(2)}, u32[]{:S(2)}) collective-permute-start(bf16[8,32,128]{2,1,0:T(8,128)(2,1)S(1)} %fusion.73), channel_id=1, source_target_pairs={{0,16},{4,20},{8,24},{12,28},{16,0},{20,4},{24,8},{28,12},{1,17},{... | collective-permute-start | bytes 196616 | tf_op jit(solution)/shard_map/ppermute | solution.py:196
  413.5 30.5 %collective-permute-start.84 = (bf16[8,32,128]{2,1,0:T(8,128)(2,1)S(1)}, bf16[8,32,128]{2,1,0:T(8,128)(2,1)S(1)}, u32[]{:S(2)}, u32[]{:S(2)}) collective-permute-start(bf16[8,32,128]{2,1,0:T(8,128)(2,1)S(1)} %fusion.69), channel_id=1, source_target_pairs={{0,16},{4,20},{8,24},{12,28},{16,0},{20,4},{24,8},{28,12},{1,17},{... | collective-permute-start | bytes 196616 | tf_op jit(solution)/shard_map/ppermute | solution.py:196
  496.6 30.0 %collective-permute-start.65 = (bf16[2,64,1024]{2,1,0:T(8,128)(2,1)S(1)}, bf16[2,64,1024]{2,1,0:T(8,128)(2,1)S(1)}, u32[]{:S(2)}, u32[]{:S(2)}) collective-permute-start(bf16[2,64,1024]{2,1,0:T(8,128)(2,1)S(1)} %dynamic-slice_bitcast_fusion.7), channel_id=1, source_target_pairs={{0,16},{4,20},{8,24},{12,28},{16,0},{20,4},{24,8},{28,12},{1,17},{... | collective-permute-start | bytes 786440 | tf_op jit(solution)/shard_map/ppermute | solution.py:196
  498.8 34.5 %collective-permute-start.73 = (bf16[2,64,1024]{2,1,0:T(8,128)(2,1)S(1)}, bf16[2,64,1024]{2,1,0:T(8,128)(2,1)S(1)}, u32[]{:S(2)}, u32[]{:S(2)}) collective-permute-start(bf16[2,64,1024]{2,1,0:T(8,128)(2,1)S(1)} %dynamic-slice_bitcast_fusion.6), channel_id=1, source_target_pairs={{0,16},{4,20},{8,24},{12,28},{16,0},{20,4},{24,8},{28,12},{1,17},{... | collective-permute-start | bytes 786440 | tf_op jit(solution)/shard_map/ppermute | solution.py:196
  509.1 29.9 %collective-permute-start.81 = (bf16[2,64,1024]{2,1,0:T(8,128)(2,1)S(1)}, bf16[2,64,1024]{2,1,0:T(8,128)(2,1)S(1)}, u32[]{:S(2)}, u32[]{:S(2)}) collective-permute-start(bf16[2,64,1024]{2,1,0:T(8,128)(2,1)S(1)} %dynamic-slice_bitcast_fusion.5), channel_id=1, source_target_pairs={{0,16},{4,20},{8,24},{12,28},{16,0},{20,4},{24,8},{28,12},{1,17},{... | collective-permute-start | bytes 786440 | tf_op jit(solution)/shard_map/ppermute | solution.py:196
  (111 other events, 1404.1 us)

commit v2 on v0

--- a/solution.py
+++ b/solution.py
@@ -3,12 +3,16 @@
 import jax
 import jax.numpy as jnp
 from jax import lax
+from jax.experimental import pallas as pl
+from jax.experimental.pallas import tpu as pltpu
 from jax.sharding import PartitionSpec as P
 
 HD = 128
 
 
 norm_epsilon = 1e-05
+
+X, CORE, ZH, ZL, Y = range(5)
 
 
 def rotary(values, positions):
@@ -58,7 +62,7 @@
     )
 
 
-def on_device(hidden, norm_gain, w_query, w_key, w_value, w_out):
+def on_device_any(hidden, norm_gain, w_query, w_key, w_value, w_out):
     rows = hidden.shape[0]
     features = hidden.shape[1] * lax.axis_size("col")
     residual = hidden.astype(jnp.float32)
@@ -71,9 +75,8 @@
     normed = lax.all_gather(scaled.astype(jnp.bfloat16), "col", axis=1, tiled=True)
     spread = lax.all_to_all(normed, "row", split_axis=1, concat_axis=0, tiled=True)
     joined = jnp.concatenate((w_query, w_key, w_value), axis=1)
-    segment = spread
     summed = lax.psum_scatter(
-        jnp.dot(segment, joined, preferred_element_type=jnp.float32).astype(jnp.bfloat16),
+        jnp.dot(spread, joined, preferred_element_type=jnp.float32).astype(jnp.bfloat16),
         "row",
         scatter_dimension=0,
         tiled=True,
@@ -101,15 +104,399 @@
     spread_context = lax.all_to_all(
         gathered_context, "row", split_axis=1, concat_axis=0, tiled=True
     )
-    segment = spread_context
     attended = lax.psum_scatter(
-        jnp.dot(segment, w_out, preferred_element_type=jnp.float32).astype(jnp.bfloat16),
+        jnp.dot(spread_context, w_out, preferred_element_type=jnp.float32).astype(jnp.bfloat16),
         "row",
         scatter_dimension=0,
         tiled=True,
     ).astype(jnp.float32)
     layer_out = (residual + attended).astype(jnp.bfloat16)
     return (context, layer_out)
+
+
+def attention_kernel(marks, q_ref, k_ref, v_ref, inv_ref, cos_ref, sin_ref, out_ref, query, keys, values):
+    half = HD // 2
+    slots, part = q_ref.shape[0], q_ref.shape[1]
+    per_row = 4
+    block = part * per_row
+    factor = math.log2(math.e) / math.sqrt(HD)
+
+    def turned(raw, at):
+        return (raw * cos_ref[at, :] + pltpu.roll(raw, half, 1) * sin_ref[at, :]).astype(
+            jnp.bfloat16
+        )
+
+    for row in range(slots // per_row):
+        zh, zl, y = row >> 2, (row >> 1) & 1, row & 1
+        for piece in range(per_row):
+            h, j = piece >> 1, piece & 1
+            slot = ((zh ^ marks[ZH]) * 2 + j) * 2 + (h ^ marks[X])
+            slot = (slot * 2 + (zl ^ marks[ZL])) * 2 + y
+            at = pl.ds(row * block + piece * part, part)
+            inverse = inv_ref[at, :]
+            query[at, :] = turned(q_ref[slot] * inverse, at)
+            keys[at, :] = turned(k_ref[slot] * inverse, at)
+            values[at, :] = (v_ref[slot] * inverse).astype(jnp.bfloat16)
+        start, stop = row * block, (row + 1) * block
+        scores = lax.dot_general(
+            query[start:stop, :],
+            keys[0:stop, :],
+            (((1,), (1,)), ((), ())),
+            preferred_element_type=jnp.float32,
+        )
+        down = lax.broadcasted_iota(jnp.int32, scores.shape, 0) + start
+        along = lax.broadcasted_iota(jnp.int32, scores.shape, 1)
+        scores = jnp.where(along <= down, scores, -jnp.inf)
+        peak = jnp.max(scores, axis=1, keepdims=True)
+        probs = jnp.exp2((scores - peak) * factor)
+        total = jnp.sum(probs, axis=1, keepdims=True)
+        weighted = jnp.dot(
+            probs.astype(jnp.bfloat16), values[0:stop, :], preferred_element_type=jnp.float32
+        )
+        context = (weighted / total).astype(jnp.bfloat16)
+        for piece in range(per_row):
+            out_ref[piece, row] = context[piece * part : (piece + 1) * part]
+
+
+def attention(marks, query, key, value, inverse):
+    slots, part, _ = query.shape
+    length = slots * part
+    half = HD // 2
+    freqs = jnp.exp(-math.log(10000.0) * 2.0 * jnp.arange(half, dtype=jnp.float32) / HD)
+    angles = jnp.arange(length, dtype=jnp.int32).astype(jnp.float32)[:, None] * freqs[None, :]
+    cosine = jnp.cos(angles)
+    sine = jnp.sin(angles)
+    whole = pl.BlockSpec(memory_space=pltpu.VMEM)
+    return pl.pallas_call(
+        attention_kernel,
+        out_shape=jax.ShapeDtypeStruct((4, slots // 4, part, HD), jnp.bfloat16),
+        in_specs=[pl.BlockSpec(memory_space=pltpu.SMEM)] + [whole] * 6,
+        out_specs=whole,
+        scratch_shapes=[pltpu.VMEM((length, HD), jnp.bfloat16)] * 3,
+        compiler_params=pltpu.CompilerParams(vmem_limit_bytes=48 * 1024 * 1024),
+        cost_estimate=pl.CostEstimate(
+            flops=2 * length * length * HD,
+            bytes_accessed=16 * length * HD,
+            transcendentals=length * length // 2,
+        ),
+    )(
+        marks,
+        query,
+        key,
+        value,
+        inverse,
+        jnp.concatenate((cosine, cosine), axis=1),
+        jnp.concatenate((-sine, sine), axis=1),
+    )
+
+
+def local_call(kernel, outputs, operands, flops=0, scratch=()):
+    whole = pl.BlockSpec(memory_space=pltpu.VMEM)
+    moved = sum(x.size * x.dtype.itemsize for x in (*operands, *outputs))
+    return pl.pallas_call(
+        kernel,
+        out_shape=tuple(outputs),
+        in_specs=[pl.BlockSpec(memory_space=pltpu.SMEM)] + [whole] * (len(operands) - 1),
+        out_specs=(whole,) * len(outputs),
+        scratch_shapes=list(scratch),
+        compiler_params=pltpu.CompilerParams(vmem_limit_bytes=48 * 1024 * 1024),
+        cost_estimate=pl.CostEstimate(flops=flops, bytes_accessed=moved, transcendentals=0),
+    )(*operands)
+
+
+def shape(like, *dims):
+    return jax.ShapeDtypeStruct(dims, like.dtype)
+
+
+def span(index, size):
+    return pl.ds(pl.multiple_of(index * size, size), size)
+
+
+def corners_kernel(marks, hidden_ref, gain_ref, own, along_y, along_x, along_xy):
+    x, y = marks[X], marks[Y]
+    rows, width = own.shape
+    for out, h, side in ((along_y, x, 1 - y), (along_x, 1 - x, y), (along_xy, 1 - x, 1 - y), (own, x, y)):
+        block = hidden_ref[span(h, rows), span(side, width)].astype(jnp.float32)
+        gain = gain_ref[:, span(side, width)].astype(jnp.float32)
+        out[...] = (block * gain).astype(out.dtype)
+
+
+def arrange_kernel(marks, v_ref, k_ref, q_ref, vk_keep, vk_send, q_keep, q_send):
+    zh, zl, y = marks[ZH], marks[ZL], marks[Y]
+
+    def head(high, middle, low):
+        return span(high * 4 + middle * 2 + low, HD)
+
+    for middle, vk_out, q_out in ((1 - zl, vk_send, q_send), (zl, vk_keep, q_keep)):
+        for i, high in enumerate((1 - y, y)):
+            for j, low in enumerate((1 - zh, zh)):
+                at = (i * 2 + j) * 2
+                vk_out[:, at * HD : (at + 1) * HD] = v_ref[:, head(high, middle, low)]
+                vk_out[:, (at + 1) * HD : (at + 2) * HD] = k_ref[:, head(high, middle, low)]
+                at = i * 2 + j
+                q_out[:, at * HD : (at + 1) * HD] = q_ref[:, head(high, middle, low)]
+
+
+def arrange_out_kernel(marks, w_ref, keep, send):
+    zh, zl = marks[ZH], marks[ZL]
+    width = keep.shape[1]
+    for out, mine in ((send, 1 - zl), (keep, zl)):
+        for i in range(2):
+            for j in range(2):
+                at = i * 2 + j
+                out[at * HD : (at + 1) * HD, :] = w_ref[
+                    span(2 * (i ^ mine) + (j ^ zh), HD), span(mine, width)
+                ]
+
+
+def project_kernel(marks, *refs):
+    keep_ref, got_ref, send_out, keep_out = refs[-4:]
+    inputs = refs[:-4]
+    middle = keep_ref.shape[1] // 2
+
+    def run(first, second):
+        for i in range(0, len(inputs), 2):
+            rows = inputs[i].shape[0]
+            at = pl.ds(i // 2 * rows, rows)
+            for out, columns in ((send_out, pl.ds(0, middle)), (keep_out, pl.ds(middle, middle))):
+                out[at, :] = (
+                    jnp.dot(inputs[i][...], first[:, columns], preferred_element_type=jnp.float32)
+                    + jnp.dot(
+                        inputs[i + 1][...], second[:, columns], preferred_element_type=jnp.float32
+                    )
+                ).astype(out.dtype)
+
+    @pl.when(marks[ZL] == marks[CORE])
+    def _():
+        run(keep_ref, got_ref)
+
+    @pl.when(marks[ZL] != marks[CORE])
+    def _():
+        run(got_ref, keep_ref)
+
+
+def project(marks, pairs, keep, got):
+    inputs = [block for pair in pairs for block in pair]
+    rows = sum(pair[0].shape[0] for pair in pairs)
+    depth, columns = keep.shape
+    outputs = (
+        jax.ShapeDtypeStruct((rows, columns // 2), jnp.bfloat16),
+        jax.ShapeDtypeStruct((rows, columns // 2), jnp.float32),
+    )
+    return local_call(
+        project_kernel, outputs, (marks, *inputs, keep, got), flops=4 * rows * depth * columns
+    )
+
+
+def out_kernel(marks, own_ref, other_ref, keep_ref, got_ref, send_0, send_1, keep_0, keep_1, joined):
+    part = own_ref.shape[-2]
+    depth = keep_ref.shape[0]
+    aside = marks[ZL] ^ marks[CORE]
+    for first in range(8):
+        order = ((first & 3) << 1) | (first >> 2)
+        row = (order ^ 7) ^ (marks[ZH] * 4 + marks[ZL] * 2 + marks[Y])
+        for h in range(2):
+            at = pl.ds((first * 2 + h) * part, part)
+            for ref, place in ((own_ref, aside), (other_ref, 1 - aside)):
+                for block in range(4):
+                    joined[at, span(place * 4 + block, HD)] = ref[h, block >> 1, block & 1, row]
+    rows, columns = send_0.shape
+    for at, outs in ((0, (send_0, send_1)), (rows, (keep_0, keep_1))):
+        for side, out in enumerate(outs):
+            across = pl.ds(side * columns, columns)
+            out[...] = (
+                jnp.dot(
+                    joined[at : at + rows, :depth],
+                    keep_ref[:, across],
+                    preferred_element_type=jnp.float32,
+                )
+                + jnp.dot(
+                    joined[at : at + rows, depth:],
+                    got_ref[:, across],
+                    preferred_element_type=jnp.float32,
+                )
+            ).astype(out.dtype)
+
+
+def home_kernel(marks, *refs):
+    out_ref = refs[-1]
+    here = marks[ZH] * 4 + marks[ZL] * 2 + marks[Y]
+    for mask, ref in enumerate(refs[:-1]):
+        peer = here ^ mask
+        head = ((peer & 1) << 2) | (peer & 2) | (peer >> 2)
+        out_ref[:, span(head, HD)] = ref[...]
+
+
+def finish_kernel(marks, hidden_ref, *refs):
+    out_ref = refs[-1]
+    rows, width = refs[0].shape
+    part = rows // 2
+    for j in range(2):
+        for place, ref in ((marks[ZL], refs[2 * j]), (1 - marks[ZL], refs[2 * j + 1])):
+            for h in range(2):
+                at = span((h ^ marks[X]) * 2 + j, part)
+                block = hidden_ref[at, span(place, width)].astype(jnp.float32)
+                added = ref[h * part : (h + 1) * part, :].astype(jnp.float32)
+                out_ref[at, span(place, width)] = (block + added).astype(out_ref.dtype)
+
+
+def after(values, *earlier):
+    return lax.optimization_barrier((values, *earlier))[0]
+
+
+def on_device_paired(hidden, norm_gain, w_query, w_key, w_value, w_out):
+    rows, cols = lax.axis_size("row"), lax.axis_size("col")
+    tokens, width = hidden.shape[0], hidden.shape[1] // 2
+    length = tokens * rows
+    row, col = lax.axis_index("row"), lax.axis_index("col")
+    y, zl, zh = row & 1, (row >> 1) & 1, row >> 2
+    core, x = col & 1, col >> 1
+    marks = jnp.stack((x, core, zh, zl, y)).astype(jnp.int32)
+    steps = {"y": (1, 0), "zl": (2, 0), "zh": (4, 0), "core": (0, 1), "x": (0, 2), "xy": (1, 2)}
+
+    def swap(values, name):
+        by_row, by_col = steps[name]
+        pairs = [
+            (r * cols + c, (r ^ by_row) * cols + (c ^ by_col))
+            for r in range(rows)
+            for c in range(cols)
+        ]
+        return lax.ppermute(values, ("row", "col"), pairs)
+
+    def ordered(mine, other, bit):
+        return jnp.where(bit == 0, mine, other), jnp.where(bit == 0, other, mine)
+
+    part = tokens // 2
+    small = part // 2
+    quarter = shape(hidden, part, width)
+    own, to_y, to_x, to_xy = local_call(
+        corners_kernel, (quarter,) * 4, (marks, hidden, norm_gain.reshape(1, -1))
+    )
+    from_xy, from_x, from_y = swap(to_xy, "xy"), swap(to_x, "x"), swap(to_y, "y")
+
+    depth = w_value.shape[0]
+    double, single = shape(w_value, depth, 8 * HD), shape(w_value, depth, 4 * HD)
+    vk_keep, vk_send, q_keep, q_send = local_call(
+        arrange_kernel,
+        (double, double, single, single),
+        (after(marks, own), w_value, w_key, w_query),
+    )
+    vk_got = swap(vk_send, "zl")
+
+    mine = jnp.stack(ordered(own, from_y, y))
+    theirs = jnp.stack(ordered(from_x, from_xy, y))
+    block, send = ordered(mine, theirs, x ^ zh)
+    landed = [block, swap(send, "zh")]
+
+    inputs = []
+    for block in landed:
+        for j in range(2):
+            held = block[:, j * small : (j + 1) * small].reshape(2 * small, width)
+            held = jnp.concatenate((held, swap(held, "zl")), axis=0)
+            held = jnp.concatenate((held, swap(held, "x")), axis=0)
+            inputs.append((held, swap(held, "core")))
+    q_got = swap(after(q_send, vk_got, inputs[1][0]), "zl")
+
+    def halves(values, axis=1):
+        middle = values.shape[axis] // 2
+        return jnp.split(values, [middle], axis=axis)
+
+    units = [((pair,), vk_keep, vk_got) for pair in inputs]
+    units += [(two, q_keep, q_got) for two in (inputs[:2], inputs[2:])]
+    sums, kept, got = [], [], []
+    for i, (pairs, first, second) in enumerate(units):
+        send, keep = project(marks, pairs, first, second)
+        if i >= 2:
+            send = after(send, sums[i - 2])
+        if i >= 4:
+            send = after(send, got[i - 4])
+        total = keep + swap(send, "y").astype(jnp.float32)
+        send, keep = halves(total)
+        sums.append(send.astype(jnp.bfloat16))
+        kept.append(keep)
+        got.append(swap(sums[-1], "zh").astype(jnp.float32))
+    results = [kept[i] + got[p] for i, p in enumerate((2, 3, 0, 1, 5, 4))]
+
+    residual = after(hidden, sums[0]).astype(jnp.float32)
+    squares = jnp.sum(residual * residual, axis=1).reshape(1, tokens)
+    squares = squares + swap(squares, "core")
+    squares = squares + swap(squares, "x")
+    for name, bit in (("y", y), ("zl", zl), ("zh", zh)):
+        squares = jnp.concatenate(ordered(squares, swap(squares, name), bit), axis=0)
+    mean = squares / (hidden.shape[1] * cols)
+    inverse = lax.rsqrt(mean + norm_epsilon).reshape(length, 1)
+
+    both = jnp.concatenate(results[:4], axis=0)
+    query = jnp.concatenate(results[4:], axis=0).reshape(-1, small, HD)
+    value = both[:, :HD].reshape(-1, small, HD)
+    key = both[:, HD:].reshape(-1, small, HD)
+    context = attention(marks, query, key, value, inverse)
+
+    out_depth, out_width = w_out.shape
+    half = shape(w_out, out_depth, out_width // 2)
+    out_keep, out_send = local_call(arrange_out_kernel, (half, half), (after(marks, q_send), w_out))
+    out_got = swap(after(out_send, q_got), "zl")
+
+    gathered, crossed = [], []
+    for j in range(2):
+        held = lax.dynamic_index_in_dim(context, x * 2 + j, 0, keepdims=False)
+        send = lax.dynamic_index_in_dim(context, (1 - x) * 2 + j, 0, keepdims=False)
+        held, send = ordered(held, swap(send, "x"), x ^ zh)
+        crossed.append(swap(send, "zh"))
+        held = jnp.stack((held, crossed[-1]))
+        held = jnp.stack((held, swap(held, "zl")))
+        held = jnp.stack((held, swap(held, "x")))
+        gathered.append((held, swap(held, "core")))
+
+    blocks = []
+    for mask in range(rows):
+        block = lax.dynamic_index_in_dim(context, row ^ mask, 1, keepdims=False)
+        if mask:
+            pairs = [(i, i ^ mask) for i in range(rows)]
+            block = lax.ppermute(after(block, crossed[1]), "row", pairs)
+        blocks.append(block.reshape(tokens, HD))
+    (context_out,) = local_call(
+        home_kernel, (shape(hidden, tokens, rows * HD),), (marks, *blocks)
+    )
+
+    sums, finals = [], []
+    for held in gathered:
+        count = rows * small
+        outputs = (jax.ShapeDtypeStruct((count, out_width // 4), jnp.bfloat16),) * 2
+        outputs += (jax.ShapeDtypeStruct((count, out_width // 4), jnp.float32),) * 2
+        products = local_call(
+            out_kernel,
+            outputs,
+            (marks, *held, out_keep, out_got),
+            flops=8 * count * out_depth * out_width,
+            scratch=[pltpu.VMEM((2 * count, 2 * out_depth), jnp.bfloat16)],
+        )
+        mine, theirs = [], []
+        for send, keep in zip(products[:2], products[2:]):
+            if len(sums) >= 2:
+                send = after(send, sums[-2])
+            total = keep + swap(send, "y").astype(jnp.float32)
+            send, keep = halves(total, 0)
+            sums.append(send.astype(jnp.bfloat16))
+            total = keep + swap(sums[-1], "zh").astype(jnp.float32)
+            send, keep = halves(total.astype(jnp.bfloat16), 0)
+            theirs.append(send)
+            mine.append(keep)
+        finals.append(jnp.concatenate(mine, axis=1))
+        finals.append(swap(jnp.concatenate(theirs, axis=1), "zl"))
+
+    (layer_out,) = local_call(
+        finish_kernel, (shape(hidden, *hidden.shape),), (marks, hidden, *finals)
+    )
+    return (context_out, layer_out)
+
+
+def on_device(hidden, norm_gain, w_query, w_key, w_value, w_out):
+    rows, cols = lax.axis_size("row"), lax.axis_size("col")
+    heads_here = w_query.shape[1] // HD
+    paired = rows == 2**3 and cols == 2**2 and heads_here == rows and hidden.shape[0] % 64 == 0
+    plan = on_device_paired if paired else on_device_any
+    return plan(hidden, norm_gain, w_query, w_key, w_value, w_out)
 
 
 def solution(mesh):

time: 797 us -> 440 us (0.55)
  waiting for transfers between devices: 536 us -> 273 us
  blocking collectives: 161 us -> 0 us
  starting transfers between devices: 0.43 us -> 64.2 us
  Pallas kernels: 0 us -> 63.3 us
  matrix products: 42.8 us -> 0 us
  between operations: 14.2 us -> 1.73 us
  local copies, waits for them, and re-layouts: 25.4 us -> 14.3 us
    reduce_scatter x2 -> x0, waiting for transfers between devices: 350 us -> none  [the longest x1 205 us: on_device(): lax.psum_scatter(jnp.dot(segment, joined, preferred_element_type=jnp.floa...]
    ppermute x0 -> x63, waiting for transfers between devices: none -> 273 us  [the longest x56 270 us: swap(): return lax.ppermute(values, ('row', 'col'), pairs)]
    all_gather x4 -> x0, waiting for transfers between devices: 185 us -> none  [the longest x1 71.7 us: on_device(): lax.all_gather(keys_here, 'row', axis=0, tiled=True)]
    all_to_all x2 -> x0, blocking collectives: 153 us -> none  [the longest x1 98.9 us: on_device(): lax.all_to_all(normed, 'row', split_axis=1, concat_axis=0, tiled=True)]
    ppermute x0 -> x63, starting transfers between devices: none -> 64.2 us  [the longest x56 54.8 us: swap(): return lax.ppermute(values, ('row', 'col'), pairs)]
    pallas_call x0 -> x14, Pallas kernels: none -> 63.3 us  [the longest x13 56.6 us: local_call(): pl.pallas_call(kernel, out_shape=tuple(outputs), in_specs=[pl.BlockSpec(m...]
    dot_general x4 -> x0, matrix products: 42.8 us -> none  [the longest x1 18.5 us: on_device(): jnp.dot(segment, joined, preferred_element_type=jnp.float32)]
    add x1 -> x18, other arithmetic: 0.01 us -> 8.82 us  [the longest x10 7.42 us: on_device_paired(): total = keep + swap(send, 'y').astype(jnp.float32)]
  transfers between devices with their start and end apart: 6 -> 63, of which waited for: 6 -> 35; matrix products, arithmetic and copies ran while one was open for 2% -> 5% of each run, Pallas kernels for 0% -> 12%
where the time goes in v2:
time: 440 us; the launch traced here: 435 us
  waiting for transfers between devices  273 us (62%)
  starting transfers between devices  64.2 us (15%)
  Pallas kernels  63.3 us (14%)
  other arithmetic  19.1 us (4%)
  local copies, waits for them, and re-layouts  14.3 us (3%)
    ppermute x56, waiting for transfers between devices, swap(): return lax.ppermute(values, ('row', 'col'), pairs)  270 us
    pallas_call x13, Pallas kernels, local_call(): pl.pallas_call(kernel, out_shape=tuple(outputs), in_specs=[pl.BlockSpec(m...  56.6 us
    ppermute x56, starting transfers between devices, swap(): return lax.ppermute(values, ('row', 'col'), pairs)  54.8 us
    unnamed x70, local copies, waits for them, and re-layouts  11.3 us
    ppermute x7, starting transfers between devices, on_device_paired(): block = lax.ppermute(after(block, crossed[1]), 'row', pairs)  9.33 us
  transfers between devices with their start and end apart: 63, of which 35 were waited for; matrix products, arithmetic and copies ran while one was open for 5% of the time, Pallas kernels for 12%

profile of v2, /device:TPU:0, one launch (start us, length us, event | category | flops | bytes accessed | tf_op | source)
XLA Modules:
  0.0 435.2 jit_solution(6050536885428827423)
XLA Ops:
  7.9 5.6 %collective-permute-done.1 = bf16[128,1024]{1,0:T(8,128)(2,1)S(1)} collective-permute-done((bf16[128,1024]{1,0:T(8,128)(2,1)S(1)}, bf16[128,1024]{1,0:T(8,128)(2,1)S(1)}, u32[]{:S(2)}, u32[]{:S(2)}) %collective-permute-start.1) | collective-permute-done | bytes 262176 | tf_op jit(solution)/shard_map/ppermute | solution.py:364
  13.5 6.1 %collective-permute-done.2 = bf16[128,1024]{1,0:T(8,128)(2,1)S(1)} collective-permute-done((bf16[128,1024]{1,0:T(8,128)(2,1)S(1)}, bf16[128,1024]{1,0:T(8,128)(2,1)S(1)}, u32[]{:S(2)}, u32[]{:S(2)}) %collective-permute-start.2) | collective-permute-done | bytes 262176 | tf_op jit(solution)/shard_map/ppermute | solution.py:364
  22.8 5.8 %shard_map.78 = (bf16[1024,1024]{1,0:T(8,128)(2,1)S(1)}, bf16[1024,1024]{1,0:T(8,128)(2,1)}, bf16[1024,512]{1,0:T(8,128)(2,1)S(1)}, bf16[1024,512]{1,0:T(8,128)(2,1)S(1)}) custom-call(s32[5]{0:T(128)S(1)} %stack.95.marks, bf16[1024,1024]{1,0:T(8,128)(2,1)} %v_ref.1, bf16[1024,1024]{1,0:T(8,128)(2,1)} %k_ref.1, bf16[1024,1024]{1,0:T(8,128)(2,1)} %q_ref.1), custom_call_target="tpu_custom_call" | custom-call | bytes 12582932 | tf_op jit(solution)/shard_map/pallas_call | solution.py:196
  35.9 5.2 %collective-permute-done.4 = bf16[256,1024]{1,0:T(8,128)(2,1)S(1)} collective-permute-done((bf16[256,1024]{1,0:T(8,128)(2,1)S(1)}, bf16[256,1024]{1,0:T(8,128)(2,1)S(1)}, u32[]{:S(2)}, u32[]{:S(2)}) %collective-permute-start.4) | collective-permute-done | bytes 524320 | tf_op jit(solution)/shard_map/ppermute | solution.py:364
  41.2 50.3 %collective-permute-done.6 = bf16[128,1024]{1,0:T(8,128)(2,1)S(1)} collective-permute-done((bf16[128,1024]{1,0:T(8,128)(2,1)S(1)}, bf16[128,1024]{1,0:T(8,128)(2,1)S(1)}, u32[]{:S(2)}, u32[]{:S(2)}) %collective-permute-start.6) | collective-permute-done | bytes 262176 | tf_op jit(solution)/shard_map/ppermute | solution.py:364
  95.4 8.6 %collective-permute-done.7 = bf16[256,1024]{1,0:T(8,128)(2,1)S(1)} collective-permute-done((bf16[256,1024]{1,0:T(8,128)(2,1)S(1)}, bf16[256,1024]{1,0:T(8,128)(2,1)S(1)}, u32[]{:S(2)}, u32[]{:S(2)}) %collective-permute-start.7) | collective-permute-done | bytes 524320 | tf_op jit(solution)/shard_map/ppermute | solution.py:364
  119.7 5.4 %shard_map.84 = (bf16[512,512]{1,0:T(8,128)(2,1)}, f32[512,512]{1,0:T(8,128)S(1)}) custom-call(s32[5]{0:T(128)S(1)} %stack.95.marks, bf16[512,1024]{1,0:T(8,128)(2,1)S(1)} %pad_maximum_fusion.2.refs_2_.refs_0_, bf16[512,1024]{1,0:T(8,128)(2,1)S(1)} %collective-permute-done.8.refs_3_.refs_1_, bf16[1024,1024]{1,0:T(8,128)(2,1)S(1)} %get-tuple-element.63.refs_2_, ...), custom_call_target="tpu_custom_call" | custom-call | flops 2147483648 | bytes 7864340 | tf_op jit(solution)/shard_map/pallas_call | solution.py:196
  145.4 5.4 %shard_map.83 = (bf16[512,512]{1,0:T(8,128)(2,1)}, f32[512,512]{1,0:T(8,128)S(1)}) custom-call(s32[5]{0:T(128)S(1)} %stack.95.marks, bf16[512,1024]{1,0:T(8,128)(2,1)} %pad_maximum_fusion.4.refs_2_.refs_0_, bf16[512,1024]{1,0:T(8,128)(2,1)} %collective-permute-done.21.refs_3_.refs_1_, bf16[1024,1024]{1,0:T(8,128)(2,1)S(1)} %copy-done.17, ...), custom_call_target="tpu_custom_call" | custom-call | flops 2147483648 | bytes 7864340 | tf_op jit(solution)/shard_map/pallas_call | solution.py:196
  151.7 18.4 %collective-permute-done.33 = f32[2,256]{1,0:T(2,128)S(1)} collective-permute-done((f32[2,256]{1,0:T(2,128)S(1)}, f32[2,256]{1,0:T(2,128)S(1)}, u32[]{:S(2)}, u32[]{:S(2)}) %collective-permute-start.33) | collective-permute-done | bytes 2080 | tf_op jit(solution)/shard_map/ppermute | solution.py:364
  185.7 12.7 %shard_map.79 = (bf16[1024,256]{1,0:T(8,128)(2,1)S(1)}, f32[1024,256]{1,0:T(8,128)S(1)}) custom-call(s32[5]{0:T(128)S(1)} %stack.95.marks, bf16[512,1024]{1,0:T(8,128)(2,1)S(1)} %copy-done.5, bf16[512,1024]{1,0:T(8,128)(2,1)S(1)} %copy-done.21, bf16[512,1024]{1,0:T(8,128)(2,1)S(1)} %copy-done.7, bf16[512,1024]{1,0:T(8,128)(2,1)S(1)} %copy-done.23, ...), custom_call_target="tpu_custom_call" | custom-call | flops 2147483648 | bytes 7864340 | tf_op jit(solution)/shard_map/pallas_call | solution.py:196
  207.4 13.0 %collective-permute-done.29 = bf16[512,256]{1,0:T(8,128)(2,1)S(1)} collective-permute-done((bf16[512,256]{1,0:T(8,128)(2,1)S(1)}, bf16[512,256]{1,0:T(8,128)(2,1)S(1)}, u32[]{:S(2)}, u32[]{:S(2)}) %collective-permute-start.29) | collective-permute-done | bytes 262176 | tf_op jit(solution)/shard_map/ppermute | solution.py:364
  229.7 14.9 %collective-permute-done.27 = bf16[1024,128]{1,0:T(8,128)(2,1)S(1)} collective-permute-done((bf16[1024,128]{1,0:T(8,128)(2,1)S(1)}, bf16[1024,128]{1,0:T(8,128)(2,1)S(1)}, u32[]{:S(2)}, u32[]{:S(2)}) %collective-permute-start.27) | collective-permute-done | bytes 262176 | tf_op jit(solution)/shard_map/ppermute | solution.py:364
  244.7 5.5 %collective-permute-done.26 = bf16[1024,128]{1,0:T(8,128)(2,1)S(1)} collective-permute-done((bf16[1024,128]{1,0:T(8,128)(2,1)S(1)}, bf16[1024,128]{1,0:T(8,128)(2,1)S(1)}, u32[]{:S(2)}, u32[]{:S(2)}) %collective-permute-start.26) | collective-permute-done | bytes 262176 | tf_op jit(solution)/shard_map/ppermute | solution.py:364
  250.3 6.7 %shard_map.85 = bf16[4,8,64,128]{3,2,1,0:T(8,128)(2,1)S(1)} custom-call(s32[5]{0:T(128)S(1)} %stack.95.marks, f32[32,64,128]{2,1,0:T(8,128)S(1)} %bitcast.81, f32[32,64,128]{2,1,0:T(8,128)S(1)} %bitcast.83, f32[32,64,128]{2,1,0:T(8,128)S(1)} %bitcast.82, f32[2048,1]{1,0:T(8,128)S(1)} %bitcast.80, f32[2048,128]{1,0:T(8,128)S(1)} %get-tuple-element.155.cos_ref, ...), custom_call_target="tpu_custom_call" | custom-call | flops 1073741824 | bytes 4194304 | tf_op jit(solution)/shard_map/pallas_call | solution.py:170
  265.5 7.3 %collective-permute-done.45 = bf16[8,64,128]{2,1,0:T(8,128)(2,1)S(1)} collective-permute-done((bf16[8,64,128]{2,1,0:T(8,128)(2,1)S(1)}, bf16[8,64,128]{2,1,0:T(8,128)(2,1)S(1)}, u32[]{:S(2)}, u32[]{:S(2)}) %collective-permute-start.45) | collective-permute-done | bytes 131104 | tf_op jit(solution)/shard_map/ppermute | solution.py:364
  272.9 8.2 %collective-permute-done.46 = bf16[2,8,64,128]{3,2,1,0:T(8,128)(2,1)S(1)} collective-permute-done((bf16[2,8,64,128]{3,2,1,0:T(8,128)(2,1)S(1)}, bf16[2,8,64,128]{3,2,1,0:T(8,128)(2,1)S(1)}, u32[]{:S(2)}, u32[]{:S(2)}) %collective-permute-start.46) | collective-permute-done | bytes 262176 | tf_op jit(solution)/shard_map/ppermute | solution.py:364
  282.9 11.3 %collective-permute-done.47 = bf16[2,2,8,64,128]{4,3,2,1,0:T(8,128)(2,1)S(1)} collective-permute-done((bf16[2,2,8,64,128]{4,3,2,1,0:T(8,128)(2,1)S(1)}, bf16[2,2,8,64,128]{4,3,2,1,0:T(8,128)(2,1)S(1)}, u32[]{:S(2)}, u32[]{:S(2)}) %collective-permute-start.47) | collective-permute-done | bytes 524320 | tf_op jit(solution)/shard_map/ppermute | solution.py:364
  295.7 11.7 %collective-permute-done.36 = bf16[8,64,128]{2,1,0:T(8,128)(2,1)S(1)} collective-permute-done((bf16[8,64,128]{2,1,0:T(8,128)(2,1)S(1)}, bf16[8,64,128]{2,1,0:T(8,128)(2,1)S(1)}, u32[]{:S(2)}, u32[]{:S(2)}) %collective-permute-start.36) | collective-permute-done | bytes 131104 | tf_op jit(solution)/shard_map/ppermute | solution.py:364
  330.3 9.6 %collective-permute-done.52 = bf16[512,512]{1,0:T(8,128)(2,1)} collective-permute-done((bf16[512,512]{1,0:T(8,128)(2,1)}, bf16[512,512]{1,0:T(8,128)(2,1)}, u32[]{:S(2)}, u32[]{:S(2)}) %collective-permute-start.52) | collective-permute-done | bytes 524320 | tf_op jit(solution)/shard_map/ppermute | solution.py:364
  357.6 6.8 %collective-permute-done.53 = bf16[256,512]{1,0:T(8,128)(2,1)S(1)} collective-permute-done((bf16[256,512]{1,0:T(8,128)(2,1)S(1)}, bf16[256,512]{1,0:T(8,128)(2,1)S(1)}, u32[]{:S(2)}, u32[]{:S(2)}) %collective-permute-start.53) | collective-permute-done | bytes 262176 | tf_op jit(solution)/shard_map/ppermute | solution.py:364
  370.2 9.0 %collective-permute-done.60 = bf16[512,512]{1,0:T(8,128)(2,1)S(1)} collective-permute-done((bf16[512,512]{1,0:T(8,128)(2,1)S(1)}, bf16[512,512]{1,0:T(8,128)(2,1)S(1)}, u32[]{:S(2)}, u32[]{:S(2)}) %collective-permute-start.60) | collective-permute-done | bytes 524320 | tf_op jit(solution)/shard_map/ppermute | solution.py:364
  379.5 8.6 %collective-permute-done.58 = bf16[512,512]{1,0:T(8,128)(2,1)S(1)} collective-permute-done((bf16[512,512]{1,0:T(8,128)(2,1)S(1)}, bf16[512,512]{1,0:T(8,128)(2,1)S(1)}, u32[]{:S(2)}, u32[]{:S(2)}) %collective-permute-start.58) | collective-permute-done | bytes 524320 | tf_op jit(solution)/shard_map/ppermute | solution.py:364
  388.2 11.1 %collective-permute-done.61 = bf16[256,512]{1,0:T(8,128)(2,1)S(1)} collective-permute-done((bf16[256,512]{1,0:T(8,128)(2,1)S(1)}, bf16[256,512]{1,0:T(8,128)(2,1)S(1)}, u32[]{:S(2)}, u32[]{:S(2)}) %collective-permute-start.61) | collective-permute-done | bytes 262176 | tf_op jit(solution)/shard_map/ppermute | solution.py:364
  399.4 14.2 %collective-permute-done.59 = bf16[256,512]{1,0:T(8,128)(2,1)S(1)} collective-permute-done((bf16[256,512]{1,0:T(8,128)(2,1)S(1)}, bf16[256,512]{1,0:T(8,128)(2,1)S(1)}, u32[]{:S(2)}, u32[]{:S(2)}) %collective-permute-start.59) | collective-permute-done | bytes 262176 | tf_op jit(solution)/shard_map/ppermute | solution.py:364
  (264 shorter events, 172.0 us)
Async XLA Ops:
  29.6 76.4 %collective-permute-start.9 = (bf16[1024,1024]{1,0:T(8,128)(2,1)}, bf16[1024,1024]{1,0:T(8,128)(2,1)S(1)}, u32[]{:S(2)}, u32[]{:S(2)}) collective-permute-start(bf16[1024,1024]{1,0:T(8,128)(2,1)} %get-tuple-element.59), channel_id=1, source_target_pairs={{0,8},{1,9},{2,10},{3,11},{4,12},{5,13},{6,14},{7,15},{8,0},{9,1},... | collective-permute-start | bytes 6291464 | tf_op jit(solution)/shard_map/ppermute | solution.py:364
  31.7 61.5 %collective-permute-start.11 = (bf16[2,128,1024]{2,1,0:T(8,128)(2,1)S(1)}, bf16[2,128,1024]{2,1,0:T(8,128)(2,1)S(1)}, u32[]{:S(2)}, u32[]{:S(2)}) collective-permute-start(bf16[2,128,1024]{2,1,0:T(8,128)(2,1)S(1)} %get-tuple-element.105), channel_id=1, source_target_pairs={{0,16},{1,17},{2,18},{3,19},{4,20},{5,21},{6,22},{7,23},{8,24},{9,... | collective-permute-start | bytes 1572872 | tf_op jit(solution)/shard_map/ppermute | solution.py:364
  34.3 57.3 %collective-permute-start.6 = (bf16[128,1024]{1,0:T(8,128)(2,1)S(1)}, bf16[128,1024]{1,0:T(8,128)(2,1)S(1)}, u32[]{:S(2)}, u32[]{:S(2)}) collective-permute-start(bf16[128,1024]{1,0:T(8,128)(2,1)S(1)} %bitcast.95), channel_id=1, source_target_pairs={{0,8},{1,9},{2,10},{3,11},{4,12},{5,13},{6,14},{7,15},{8,0},{9,1},... | collective-permute-start | bytes 786440 | tf_op jit(solution)/shard_map/ppermute | solution.py:364
  41.2 64.9 %collective-permute-start.5 = (bf16[512,1024]{1,0:T(8,128)(2,1)S(1)}, bf16[512,1024]{1,0:T(8,128)(2,1)S(1)}, u32[]{:S(2)}, u32[]{:S(2)}) collective-permute-start(bf16[512,1024]{1,0:T(8,128)(2,1)S(1)} %pad_maximum_fusion.1.refs_0_), channel_id=1, source_target_pairs={{0,1},{1,0},{2,3},{3,2},{4,5},{5,4},{6,7},{7,6},{8,9},{9,8},{10,11... | collective-permute-start | bytes 3145736 | tf_op jit(solution)/shard_map/ppermute | solution.py:364
  93.7 21.8 %collective-permute-start.12 = (bf16[128,1024]{1,0:T(8,128)(2,1)S(1)}, bf16[128,1024]{1,0:T(8,128)(2,1)S(1)}, u32[]{:S(2)}, u32[]{:S(2)}) collective-permute-start(bf16[128,1024]{1,0:T(8,128)(2,1)S(1)} %bitcast.92), channel_id=1, source_target_pairs={{0,8},{1,9},{2,10},{3,11},{4,12},{5,13},{6,14},{7,15},{8,0},{9,1},... | collective-permute-start | bytes 786440 | tf_op jit(solution)/shard_map/ppermute | solution.py:364
  119.6 24.0 %collective-permute-start.21 = (bf16[512,1024]{1,0:T(8,128)(2,1)}, bf16[512,1024]{1,0:T(8,128)(2,1)}, u32[]{:S(2)}, u32[]{:S(2)}) collective-permute-start(bf16[512,1024]{1,0:T(8,128)(2,1)} %pad_maximum_fusion.4.refs_2_.refs_0_), channel_id=1, source_target_pairs={{0,1},{1,0},{2,3},{3,2},{4,5},{5,4},{6,7},{7,6},{8,9},{9,8},{10,11... | collective-permute-start | bytes 3145736 | tf_op jit(solution)/shard_map/ppermute | solution.py:364
  132.9 38.1 %collective-permute-start.14 = (bf16[512,1024]{1,0:T(8,128)(2,1)S(1)}, bf16[512,1024]{1,0:T(8,128)(2,1)S(1)}, u32[]{:S(2)}, u32[]{:S(2)}) collective-permute-start(bf16[512,1024]{1,0:T(8,128)(2,1)S(1)} %pad_maximum_fusion.3.refs_0_), channel_id=1, source_target_pairs={{0,1},{1,0},{2,3},{3,2},{4,5},{5,4},{6,7},{7,6},{8,9},{9,8},{10,11... | collective-permute-start | bytes 3145736 | tf_op jit(solution)/shard_map/ppermute | solution.py:364
  133.0 46.7 %collective-permute-start.10 = (bf16[1024,512]{1,0:T(8,128)(2,1)}, bf16[1024,512]{1,0:T(8,128)(2,1)}, u32[]{:S(2)}, u32[]{:S(2)}) collective-permute-start(bf16[1024,512]{1,0:T(8,128)(2,1)} %copy-done.19), channel_id=1, source_target_pairs={{0,8},{1,9},{2,10},{3,11},{4,12},{5,13},{6,14},{7,15},{8,0},{9,1},... | collective-permute-start | bytes 3145736 | tf_op jit(solution)/shard_map/ppermute | solution.py:364
  133.3 74.0 %collective-permute-start.17 = (bf16[512,256]{1,0:T(8,128)(2,1)}, bf16[512,256]{1,0:T(8,128)(2,1)S(1)}, u32[]{:S(2)}, u32[]{:S(2)}) collective-permute-start(bf16[512,256]{1,0:T(8,128)(2,1)} %split.187), channel_id=1, source_target_pairs={{0,16},{1,17},{2,18},{3,19},{4,20},{5,21},{6,22},{7,23},{8,24},{9,... | collective-permute-start | bytes 786440 | tf_op jit(solution)/shard_map/ppermute | solution.py:364
  143.4 61.7 %collective-permute-start.24 = (bf16[512,256]{1,0:T(8,128)(2,1)}, bf16[512,256]{1,0:T(8,128)(2,1)}, u32[]{:S(2)}, u32[]{:S(2)}) collective-permute-start(bf16[512,256]{1,0:T(8,128)(2,1)} %split.185), channel_id=1, source_target_pairs={{0,16},{1,17},{2,18},{3,19},{4,20},{5,21},{6,22},{7,23},{8,24},{9,... | collective-permute-start | bytes 786440 | tf_op jit(solution)/shard_map/ppermute | solution.py:364
  143.6 26.6 %collective-permute-start.33 = (f32[2,256]{1,0:T(2,128)S(1)}, f32[2,256]{1,0:T(2,128)S(1)}, u32[]{:S(2)}, u32[]{:S(2)}) collective-permute-start(f32[2,256]{1,0:T(2,128)S(1)} %pad_maximum_fusion.25), channel_id=1, source_target_pairs={{0,8},{1,9},{2,10},{3,11},{4,12},{5,13},{6,14},{7,15},{8,0},{9,1},... | collective-permute-start | bytes 6152 | tf_op jit(solution)/shard_map/ppermute | solution.py:364
  170.2 28.3 %collective-permute-start.23 = (bf16[512,512]{1,0:T(8,128)(2,1)}, bf16[512,512]{1,0:T(8,128)(2,1)}, u32[]{:S(2)}, u32[]{:S(2)}) collective-permute-start(bf16[512,512]{1,0:T(8,128)(2,1)} %get-tuple-element.77), channel_id=1, source_target_pairs={{0,4},{1,5},{2,6},{3,7},{4,0},{5,1},{6,2},{7,3},{8,12},{9,13},{10,... | collective-permute-start | bytes 1572872 | tf_op jit(solution)/shard_map/ppermute | solution.py:364
  177.2 26.2 %collective-permute-start.16 = (bf16[512,512]{1,0:T(8,128)(2,1)}, bf16[512,512]{1,0:T(8,128)(2,1)}, u32[]{:S(2)}, u32[]{:S(2)}) collective-permute-start(bf16[512,512]{1,0:T(8,128)(2,1)} %get-tuple-element.68), channel_id=1, source_target_pairs={{0,4},{1,5},{2,6},{3,7},{4,0},{5,1},{6,2},{7,3},{8,12},{9,13},{10,... | collective-permute-start | bytes 1572872 | tf_op jit(solution)/shard_map/ppermute | solution.py:364
  202.5 24.4 %collective-permute-start.25 = (bf16[1024,256]{1,0:T(8,128)(2,1)S(1)}, bf16[1024,256]{1,0:T(8,128)(2,1)S(1)}, u32[]{:S(2)}, u32[]{:S(2)}) collective-permute-start(bf16[1024,256]{1,0:T(8,128)(2,1)S(1)} %get-tuple-element.79), channel_id=1, source_target_pairs={{0,4},{1,5},{2,6},{3,7},{4,0},{5,1},{6,2},{7,3},{8,12},{9,13},{10,... | collective-permute-start | bytes 1572872 | tf_op jit(solution)/shard_map/ppermute | solution.py:364
  205.0 21.1 %collective-permute-start.18 = (bf16[1024,256]{1,0:T(8,128)(2,1)S(1)}, bf16[1024,256]{1,0:T(8,128)(2,1)S(1)}, u32[]{:S(2)}, u32[]{:S(2)}) collective-permute-start(bf16[1024,256]{1,0:T(8,128)(2,1)S(1)} %get-tuple-element.70), channel_id=1, source_target_pairs={{0,4},{1,5},{2,6},{3,7},{4,0},{5,1},{6,2},{7,3},{8,12},{9,13},{10,... | collective-permute-start | bytes 1572872 | tf_op jit(solution)/shard_map/ppermute | solution.py:364
  227.1 23.0 %collective-permute-start.26 = (bf16[1024,128]{1,0:T(8,128)(2,1)S(1)}, bf16[1024,128]{1,0:T(8,128)(2,1)S(1)}, u32[]{:S(2)}, u32[]{:S(2)}) collective-permute-start(bf16[1024,128]{1,0:T(8,128)(2,1)S(1)} %split.183), channel_id=1, source_target_pairs={{0,16},{1,17},{2,18},{3,19},{4,20},{5,21},{6,22},{7,23},{8,24},{9,... | collective-permute-start | bytes 786440 | tf_op jit(solution)/shard_map/ppermute | solution.py:364
  282.5 34.2 %collective-permute-start.49 = (bf16[512,1024]{1,0:T(8,128)(2,1)S(1)}, bf16[512,1024]{1,0:T(8,128)(2,1)S(1)}, u32[]{:S(2)}, u32[]{:S(2)}) collective-permute-start(bf16[512,1024]{1,0:T(8,128)(2,1)S(1)} %get-tuple-element.91), channel_id=1, source_target_pairs={{0,8},{1,9},{2,10},{3,11},{4,12},{5,13},{6,14},{7,15},{8,0},{9,1},... | collective-permute-start | bytes 3145736 | tf_op jit(solution)/shard_map/ppermute | solution.py:364
  294.3 22.5 %collective-permute-start.48 = (bf16[2,2,2,8,64,128]{5,4,3,2,1,0:T(8,128)(2,1)S(1)}, bf16[2,2,2,8,64,128]{5,4,3,2,1,0:T(8,128)(2,1)S(1)}, u32[]{:S(2)}, u32[]{:S(2)}) collective-permute-start(bf16[2,2,2,8,64,128]{5,4,3,2,1,0:T(8,128)(2,1)S(1)} %pad_maximum_fusion.8.own_ref), channel_id=1, source_target_pairs={{0,1},{1,0},{2,3},{3,2},{4,5},{5,4},{6,7},{7,6},{8,9},{9,8},{10,11... | collective-permute-start | bytes 3145736 | tf_op jit(solution)/shard_map/ppermute | solution.py:364
  326.7 24.7 %collective-permute-start.57 = (bf16[2,2,2,8,64,128]{5,4,3,2,1,0:T(8,128)(2,1)S(1)}, bf16[2,2,2,8,64,128]{5,4,3,2,1,0:T(8,128)(2,1)}, u32[]{:S(2)}, u32[]{:S(2)}) collective-permute-start(bf16[2,2,2,8,64,128]{5,4,3,2,1,0:T(8,128)(2,1)S(1)} %pad_maximum_fusion.9.own_ref), channel_id=1, source_target_pairs={{0,1},{1,0},{2,3},{3,2},{4,5},{5,4},{6,7},{7,6},{8,9},{9,8},{10,11... | collective-permute-start | bytes 3145736 | tf_op jit(solution)/shard_map/ppermute | solution.py:364
  326.7 21.8 %collective-permute-start.50 = (bf16[512,512]{1,0:T(8,128)(2,1)S(1)}, bf16[512,512]{1,0:T(8,128)(2,1)}, u32[]{:S(2)}, u32[]{:S(2)}) collective-permute-start(bf16[512,512]{1,0:T(8,128)(2,1)S(1)} %get-tuple-element.93), channel_id=1, source_target_pairs={{0,4},{1,5},{2,6},{3,7},{4,0},{5,1},{6,2},{7,3},{8,12},{9,13},{10,... | collective-permute-start | bytes 1572872 | tf_op jit(solution)/shard_map/ppermute | solution.py:364
  327.7 86.2 %collective-permute-start.37 = (bf16[4,64,128]{2,1,0:T(8,128)(2,1)S(1)}, bf16[4,64,128]{2,1,0:T(8,128)(2,1)S(1)}, u32[]{:S(2)}, u32[]{:S(2)}) collective-permute-start(bf16[4,64,128]{2,1,0:T(8,128)(2,1)S(1)} %get-tuple-element.81), channel_id=1, source_target_pairs={{0,4},{4,0},{8,12},{12,8},{16,20},{20,16},{24,28},{28,24},{1,5},{5... | collective-permute-start | bytes 196616 | tf_op jit(solution)/shard_map/ppermute | solution.py:456
  328.9 86.4 %collective-permute-start.38 = (bf16[4,64,128]{2,1,0:T(8,128)(2,1)S(1)}, bf16[4,64,128]{2,1,0:T(8,128)(2,1)S(1)}, u32[]{:S(2)}, u32[]{:S(2)}) collective-permute-start(bf16[4,64,128]{2,1,0:T(8,128)(2,1)S(1)} %get-tuple-element.82), channel_id=1, source_target_pairs={{0,8},{4,12},{8,0},{12,4},{16,24},{20,28},{24,16},{28,20},{1,9},{5... | collective-permute-start | bytes 196616 | tf_op jit(solution)/shard_map/ppermute | solution.py:456
  339.9 78.3 %collective-permute-start.39 = (bf16[4,64,128]{2,1,0:T(8,128)(2,1)S(1)}, bf16[4,64,128]{2,1,0:T(8,128)(2,1)S(1)}, u32[]{:S(2)}, u32[]{:S(2)}) collective-permute-start(bf16[4,64,128]{2,1,0:T(8,128)(2,1)S(1)} %get-tuple-element.83), channel_id=1, source_target_pairs={{0,12},{4,8},{8,4},{12,0},{16,28},{20,24},{24,20},{28,16},{1,13},{... | collective-permute-start | bytes 196616 | tf_op jit(solution)/shard_map/ppermute | solution.py:456
  379.2 39.3 %collective-permute-start.40 = (bf16[4,64,128]{2,1,0:T(8,128)(2,1)S(1)}, bf16[4,64,128]{2,1,0:T(8,128)(2,1)S(1)}, u32[]{:S(2)}, u32[]{:S(2)}) collective-permute-start(bf16[4,64,128]{2,1,0:T(8,128)(2,1)S(1)} %get-tuple-element.84), channel_id=1, source_target_pairs={{0,16},{4,20},{8,24},{12,28},{16,0},{20,4},{24,8},{28,12},{1,17},{... | collective-permute-start | bytes 196616 | tf_op jit(solution)/shard_map/ppermute | solution.py:456
  (73 other events, 944.2 us)

commit v3 on v0

--- a/solution.py
+++ b/solution.py
@@ -1,14 +1,19 @@
+import functools
 import math
 
 import jax
 import jax.numpy as jnp
 from jax import lax
+from jax.experimental import pallas as pl
+from jax.experimental.pallas import tpu as pltpu
 from jax.sharding import PartitionSpec as P
 
 HD = 128
 
 
 norm_epsilon = 1e-05
+
+X, CORE, ZH, ZL, Y = range(5)
 
 
 def rotary(values, positions):
@@ -58,7 +63,7 @@
     )
 
 
-def on_device(hidden, norm_gain, w_query, w_key, w_value, w_out):
+def on_device_any(hidden, norm_gain, w_query, w_key, w_value, w_out):
     rows = hidden.shape[0]
     features = hidden.shape[1] * lax.axis_size("col")
     residual = hidden.astype(jnp.float32)
@@ -71,9 +76,8 @@
     normed = lax.all_gather(scaled.astype(jnp.bfloat16), "col", axis=1, tiled=True)
     spread = lax.all_to_all(normed, "row", split_axis=1, concat_axis=0, tiled=True)
     joined = jnp.concatenate((w_query, w_key, w_value), axis=1)
-    segment = spread
     summed = lax.psum_scatter(
-        jnp.dot(segment, joined, preferred_element_type=jnp.float32).astype(jnp.bfloat16),
+        jnp.dot(spread, joined, preferred_element_type=jnp.float32).astype(jnp.bfloat16),
         "row",
         scatter_dimension=0,
         tiled=True,
@@ -101,15 +105,412 @@
     spread_context = lax.all_to_all(
         gathered_context, "row", split_axis=1, concat_axis=0, tiled=True
     )
-    segment = spread_context
     attended = lax.psum_scatter(
-        jnp.dot(segment, w_out, preferred_element_type=jnp.float32).astype(jnp.bfloat16),
+        jnp.dot(spread_context, w_out, preferred_element_type=jnp.float32).astype(jnp.bfloat16),
         "row",
         scatter_dimension=0,
         tiled=True,
     ).astype(jnp.float32)
     layer_out = (residual + attended).astype(jnp.bfloat16)
     return (context, layer_out)
+
+
+def attention_kernel(marks, q_ref, k_ref, v_ref, cos_ref, sin_ref, out_ref, query, keys, values):
+    half = HD // 2
+    slots, part = q_ref.shape[0], q_ref.shape[1]
+    block = part * 2
+    pieces = out_ref.shape[0]
+    small = block // pieces
+    factor = math.log2(math.e) / math.sqrt(HD)
+
+    def turned(raw, at):
+        return (raw * cos_ref[at, :] + pltpu.roll(raw, half, 1) * sin_ref[at, :]).astype(
+            jnp.bfloat16
+        )
+
+    for row in range(slots // 2):
+        zh, zl, y = row >> 2, (row >> 1) & 1, row & 1
+        for h in range(2):
+            slot = (zh ^ marks[ZH]) * 2 + (h ^ marks[X])
+            slot = (slot * 2 + (zl ^ marks[ZL])) * 2 + y
+            at = pl.ds(row * block + h * part, part)
+            query[at, :] = turned(q_ref[slot], at)
+            keys[at, :] = turned(k_ref[slot], at)
+            values[at, :] = v_ref[slot].astype(jnp.bfloat16)
+        start, stop = row * block, (row + 1) * block
+        scores = lax.dot_general(
+            query[start:stop, :],
+            keys[0:stop, :],
+            (((1,), (1,)), ((), ())),
+            preferred_element_type=jnp.float32,
+        )
+        down = lax.broadcasted_iota(jnp.int32, scores.shape, 0) + start
+        along = lax.broadcasted_iota(jnp.int32, scores.shape, 1)
+        scores = jnp.where(along <= down, scores, -jnp.inf)
+        peak = jnp.max(scores, axis=1, keepdims=True)
+        probs = jnp.exp2((scores - peak) * factor)
+        total = jnp.sum(probs, axis=1, keepdims=True)
+        weighted = jnp.dot(
+            probs.astype(jnp.bfloat16), values[0:stop, :], preferred_element_type=jnp.float32
+        )
+        context = (weighted / total).astype(jnp.bfloat16)
+        for piece in range(pieces):
+            out_ref[piece, row] = context[piece * small : (piece + 1) * small]
+
+
+def turning(positions):
+    half = HD // 2
+    freqs = jnp.exp(-math.log(10000.0) * 2.0 * jnp.arange(half, dtype=jnp.float32) / HD)
+    angles = positions.astype(jnp.float32)[:, None] * freqs[None, :]
+    cosine = jnp.cos(angles)
+    sine = jnp.sin(angles)
+    return jnp.concatenate((cosine, cosine), axis=1), jnp.concatenate((-sine, sine), axis=1)
+
+
+def attention(marks, query, key, value, cosine, sine):
+    slots, part, _ = query.shape
+    length = slots * part
+    (context,) = local_call(
+        attention_kernel,
+        (jax.ShapeDtypeStruct((4, slots // 2, part // 2, HD), jnp.bfloat16),),
+        (marks, query, key, value, cosine, sine),
+        scratch=[jax.ShapeDtypeStruct((length, HD), jnp.bfloat16)] * 3,
+        spare=12,
+    )
+    return context
+
+
+def local_call(kernel, outputs, operands, scratch=(), spare=4):
+    whole = pl.BlockSpec(memory_space=pltpu.VMEM)
+    needed = sum(max(x.size, 1024) * x.dtype.itemsize for x in (*operands, *outputs, *scratch))
+    return pl.pallas_call(
+        kernel,
+        name=getattr(kernel, "__name__", "corners_kernel"),
+        out_shape=tuple(outputs),
+        in_specs=[pl.BlockSpec(memory_space=pltpu.SMEM)] + [whole] * (len(operands) - 1),
+        out_specs=(whole,) * len(outputs),
+        scratch_shapes=[pltpu.VMEM(x.shape, x.dtype) for x in scratch],
+        compiler_params=pltpu.CompilerParams(vmem_limit_bytes=needed + spare * 1024 * 1024),
+        cost_estimate=pl.CostEstimate(flops=1, bytes_accessed=1, transcendentals=0),
+    )(*operands)
+
+
+def shape(like, *dims):
+    return jax.ShapeDtypeStruct(dims, like.dtype)
+
+
+def span(index, size):
+    return pl.ds(pl.multiple_of(index * size, size), size)
+
+
+def squares_kernel(marks, hidden_ref, out_ref):
+    values = hidden_ref[...].astype(jnp.float32)
+    total = jnp.sum(values * values, axis=1, keepdims=True)
+    out_ref[...] = jnp.broadcast_to(total, out_ref.shape)
+
+
+def corners_kernel(features, marks, hidden_ref, gain_ref, sum_0, sum_1, along_xy, along_x, along_y, own):
+    x, y = marks[X], marks[Y]
+    rows, width = own.shape
+    places = ((1 - x, 1 - y), (1 - x, y), (x, 1 - y), (x, y))
+    for out, (h, side) in zip((along_xy, along_x, along_y, own), places):
+        block = hidden_ref[span(h, rows), span(side, width)].astype(jnp.float32)
+        gain = gain_ref[:, span(side, width)].astype(jnp.float32)
+        mean = (sum_0[span(h, rows), 0:1] + sum_1[span(h, rows), 0:1]) / features
+        out[...] = (block * lax.rsqrt(mean + norm_epsilon) * gain).astype(out.dtype)
+
+
+def arrange_kernel(marks, w_ref, keep, send):
+    zh, zl, y = marks[ZH], marks[ZL], marks[Y]
+    for middle, out in ((1 - zl, send), (zl, keep)):
+        for i, high in enumerate((1 - y, y)):
+            for j, low in enumerate((1 - zh, zh)):
+                at = (i * 2 + j) * HD
+                out[:, at : at + HD] = w_ref[:, span(high * 4 + middle * 2 + low, HD)]
+
+
+def arrange_out_kernel(marks, w_ref, keep, send):
+    zh, zl = marks[ZH], marks[ZL]
+    width = keep.shape[1]
+    for out, mine in ((send, 1 - zl), (keep, zl)):
+        for i in range(2):
+            for j in range(2):
+                at = i * 2 + j
+                out[at * HD : (at + 1) * HD, :] = w_ref[
+                    span(2 * (i ^ mine) + (j ^ zh), HD), span(mine, width)
+                ]
+
+
+def project_kernel(marks, *refs):
+    first, second, send_out, keep_out = refs[-4:]
+    inputs = refs[:-4]
+    middle = first.shape[1] // 2
+    for i in range(0, len(inputs), 2):
+        rows = inputs[i].shape[0]
+        into = pl.ds(i // 2 * rows, rows)
+        for out, columns in ((send_out, pl.ds(0, middle)), (keep_out, pl.ds(middle, middle))):
+            out[into, :] = (
+                jnp.dot(inputs[i][...], first[:, columns], preferred_element_type=jnp.float32)
+                + jnp.dot(
+                    inputs[i + 1][...], second[:, columns], preferred_element_type=jnp.float32
+                )
+            ).astype(out.dtype)
+
+
+def project(marks, pairs, first, second):
+    inputs = [block for pair in pairs for block in pair]
+    rows = sum(pair[0].shape[0] for pair in pairs)
+    columns = first.shape[1]
+    outputs = (
+        jax.ShapeDtypeStruct((rows, columns // 2), jnp.bfloat16),
+        jax.ShapeDtypeStruct((rows, columns // 2), jnp.float32),
+    )
+    return local_call(project_kernel, outputs, (marks, *inputs, first, second))
+
+
+def out_kernel(
+    marks, own_0, own_1, other_0, other_1, keep_ref, got_ref, send_0, send_1, keep_0, keep_1, joined
+):
+    part = own_0.shape[-2]
+    depth = keep_ref.shape[0]
+    aside = marks[ZL] ^ marks[CORE]
+    for first in range(8):
+        order = ((first & 3) << 1) | (first >> 2)
+        row = (order ^ 7) ^ (marks[ZH] * 4 + marks[ZL] * 2 + marks[Y])
+        for h, (own, other) in enumerate(((own_0, other_0), (own_1, other_1))):
+            at = pl.ds((first * 2 + h) * part, part)
+            for ref, place in ((own, aside), (other, 1 - aside)):
+                for block in range(4):
+                    joined[at, span(place * 4 + block, HD)] = ref[block >> 1, block & 1, row]
+    rows, columns = send_0.shape
+    for at, outs in ((0, (send_0, send_1)), (rows, (keep_0, keep_1))):
+        for side, out in enumerate(outs):
+            across = pl.ds(side * columns, columns)
+            out[...] = (
+                jnp.dot(
+                    joined[at : at + rows, :depth],
+                    keep_ref[:, across],
+                    preferred_element_type=jnp.float32,
+                )
+                + jnp.dot(
+                    joined[at : at + rows, depth:],
+                    got_ref[:, across],
+                    preferred_element_type=jnp.float32,
+                )
+            ).astype(out.dtype)
+
+
+def home_kernel(marks, keep_ref, got_ref, out_ref):
+    pieces, small = keep_ref.shape[2:4]
+    for aside, ref in enumerate((keep_ref, got_ref)):
+        for block in range(4):
+            zl, zh = block >> 1, block & 1
+            head = (marks[Y] ^ aside) * 4 + (marks[ZL] ^ zl) * 2 + (marks[ZH] ^ zh)
+            for piece in range(pieces):
+                out_ref[piece * small : (piece + 1) * small, span(head, HD)] = ref[zl, zh, piece]
+
+
+def finish_kernel(marks, hidden_ref, *refs):
+    out_ref = refs[-1]
+    rows, width = refs[0].shape
+    part = rows // 2
+    for j in range(2):
+        for place, ref in ((marks[ZL], refs[2 * j]), (1 - marks[ZL], refs[2 * j + 1])):
+            for h in range(2):
+                at = span((h ^ marks[X]) * 2 + j, part)
+                block = hidden_ref[at, span(place, width)].astype(jnp.float32)
+                added = ref[h * part : (h + 1) * part, :].astype(jnp.float32)
+                out_ref[at, span(place, width)] = (block + added).astype(out_ref.dtype)
+
+
+def after(values, *earlier):
+    return lax.optimization_barrier((values, *earlier))[0]
+
+
+def on_device_paired(hidden, norm_gain, w_query, w_key, w_value, w_out):
+    rows, cols = lax.axis_size("row"), lax.axis_size("col")
+    tokens, width = hidden.shape[0], hidden.shape[1] // 2
+    length = tokens * rows
+    row, col = lax.axis_index("row"), lax.axis_index("col")
+    y, zl, zh = row & 1, (row >> 1) & 1, row >> 2
+    core, x = col & 1, col >> 1
+    marks = jnp.stack((x, core, zh, zl, y)).astype(jnp.int32)
+    steps = {"y": (1, 0), "zl": (2, 0), "zh": (4, 0), "core": (0, 1), "x": (0, 2), "xy": (1, 2)}
+
+    def swap(values, name):
+        by_row, by_col = steps[name]
+        pairs = [
+            (r * cols + c, (r ^ by_row) * cols + (c ^ by_col))
+            for r in range(rows)
+            for c in range(cols)
+        ]
+        return lax.ppermute(values, ("row", "col"), pairs)
+
+    def spread(block, along, *earlier):
+        held = jnp.concatenate((block, along))
+        beside = swap(after(held, *earlier), "x")
+        return held, swap(held, "core"), beside
+
+    def ordered(mine, other, bit):
+        return jnp.where(bit == 0, mine, other), jnp.where(bit == 0, other, mine)
+
+    def index(values, at, axis=0):
+        return lax.dynamic_index_in_dim(values, at, axis, keepdims=False)
+
+    def halves(values):
+        middle = values.shape[0] // 2
+        return values[:middle], values[middle:]
+
+    sums_shape = jax.ShapeDtypeStruct((tokens, HD), jnp.float32)
+    (squares,) = local_call(squares_kernel, (sums_shape,), (marks, hidden))
+    depth = w_value.shape[0]
+
+    def arranged(weight, *earlier):
+        half = shape(weight, depth, 4 * HD)
+        return local_call(arrange_kernel, (half, half), (after(marks, *earlier), weight))
+
+    v_keep, v_send = arranged(w_value)
+    v_got = swap(v_send, "zl")
+    squares = squares + swap(squares, "core")
+    squares = after(squares, v_send)
+    squares_x = swap(squares, "x")
+
+    quarter = shape(hidden, tokens // 2, width)
+    to_xy, to_x, to_y, own = local_call(
+        functools.partial(corners_kernel, hidden.shape[1] * cols),
+        (quarter,) * 4,
+        (marks, hidden, norm_gain.reshape(1, -1), squares, squares_x),
+    )
+    from_xy, from_x, from_y = swap(to_xy, "xy"), swap(to_x, "x"), swap(to_y, "y")
+
+    mine = jnp.concatenate(ordered(own, from_y, y))
+    theirs = jnp.concatenate(ordered(from_x, from_xy, y))
+    block_a, send = ordered(mine, theirs, x ^ zh)
+    along_a = swap(after(block_a, v_got), "zl")
+    block_b = swap(after(send, along_a), "zh")
+
+    k_keep, k_send = arranged(w_key, to_y)
+    q_keep, q_send = arranged(w_query, to_y)
+    positions = jnp.arange(length, dtype=jnp.int32)
+    cosine, sine = turning(after(positions, to_y))
+    out_depth, out_width = w_out.shape
+    half = shape(w_out, out_depth, out_width // 2)
+    out_keep, out_send = local_call(arrange_out_kernel, (half, half), (after(marks, to_y), w_out))
+
+    along_a = after(along_a, k_send, q_send, cosine, sine, out_send)
+    k_got = swap(after(k_send, along_a), "zl")
+    held_a, core_a, beside_a = spread(block_a, along_a)
+    pairs_a = ((held_a, core_a), (beside_a, swap(beside_a, "core")))
+    along_b = swap(block_b, "zl")
+    held_b, core_b, beside_b = spread(block_b, along_b, beside_a)
+    q_got = swap(after(q_send, k_got), "zl")
+
+    def multiply(pairs, keep, got, *earlier):
+        return project(after(marks, *earlier), pairs, *ordered(keep, got, zl ^ core))
+
+    weights = ((v_keep, v_got), (k_keep, k_got), (q_keep, q_got))
+    products = [multiply(pairs_a, *weights[0])]
+    products.append(multiply(pairs_a, *weights[1], products[0][0]))
+    sums, kept, got = [], [], []
+    for i in range(6):
+        if i == 1:
+            products.append(multiply(pairs_a, *weights[2], sums[0]))
+            beside_b = after(beside_b, sums[0])
+            pairs_b = ((held_b, core_b), (beside_b, swap(beside_b, "core")))
+        if 2 <= i < 5:
+            products.append(multiply(pairs_b, *weights[i - 2], sums[i - 1]))
+        send, keep = products[i]
+        if i >= 2:
+            send = after(send, sums[i - 2])
+            keep = after(keep, got[i - 2])
+        if i < 5:
+            keep = after(keep, products[i + 1][0])
+        total = keep + swap(send, "y").astype(jnp.float32)
+        sums.append(total[:, :HD].astype(jnp.bfloat16))
+        kept.append(total[:, HD:])
+        got.append(swap(sums[-1], "zh"))
+
+    value, key, query = (
+        jnp.concatenate((kept[a] + got[b].astype(jnp.float32), kept[b] + got[a].astype(jnp.float32)))
+        .reshape(-1, tokens // 2, HD)
+        for a, b in ((0, 3), (1, 4), (2, 5))
+    )
+    context = attention(marks, query, key, value, cosine, sine)
+    pieces, _, small, _ = context.shape
+
+    out_got = swap(after(out_send, q_got), "zl")
+    context = after(context, out_got)
+
+    sides = context.reshape(2, pieces // 2, rows, small, HD)
+    outward = index(sides, 1 - x)
+    held, crossed = [], []
+    for j in range(pieces // 2):
+        near, send = ordered(index(sides, x)[j], swap(outward[j], "x"), x ^ zh)
+        held.append(near)
+        crossed.append(swap(send, "zh"))
+    blocks = [jnp.stack((held[j], crossed[j])) for j in range(pieces // 2)]
+    alongs = [swap(block, "zl") for block in blocks]
+    sums, got, mine, theirs, finals = [], [], [], [], []
+    count = rows * small
+    outputs = (jax.ShapeDtypeStruct((count, out_width // 4), jnp.bfloat16),) * 2
+    outputs += (jax.ShapeDtypeStruct((count, out_width // 4), jnp.float32),) * 2
+    products = []
+    for block, along in zip(blocks, alongs):
+        block = jnp.stack((block, along))
+        beside = swap(block, "x")
+        further = swap(after(beside, alongs[-1], *(sent[0] for sent in products)), "core")
+        products.append(
+            local_call(
+                out_kernel,
+                outputs,
+                (marks, block, beside, swap(block, "core"), further, out_keep, out_got),
+                scratch=[jax.ShapeDtypeStruct((2 * count, 2 * out_depth), jnp.bfloat16)],
+            )
+        )
+    first, second = products
+    block = after(context, first[0]).reshape(pieces, 2, 2, 2, small, HD)
+    home = jnp.stack((index(block, zh, 1), swap(index(block, 1 - zh, 1), "zh")))
+    for i, (send, keep) in enumerate(
+        ((first[0], first[2]), (first[1], first[3]), (second[0], second[2]), (second[1], second[3]))
+    ):
+        if i == 0:
+            keep = after(keep, home)
+        if i == 3:
+            home = jnp.stack((index(home, zl, 2), swap(index(home, 1 - zl, 2), "zl")))
+            keep = after(keep, home)
+        if i >= 2:
+            send = after(send, sums[i - 2])
+        if i >= 3:
+            send = after(send, got[i - 3])
+        total = keep + swap(send, "y").astype(jnp.float32)
+        send, keep = halves(total)
+        sums.append(send.astype(jnp.bfloat16))
+        got.append(swap(sums[-1], "zh"))
+        send, keep = halves((keep + got[-1].astype(jnp.float32)).astype(jnp.bfloat16))
+        theirs.append(send)
+        mine.append(keep)
+        if i & 1:
+            finals.append(jnp.concatenate(mine[-2:], axis=1))
+            finals.append(swap(jnp.concatenate(theirs[-2:], axis=1), "zl"))
+
+    home = after(home, sums[3])
+    (context_out,) = local_call(
+        home_kernel,
+        (shape(hidden, tokens, rows * HD),),
+        (marks, index(home, y, 3), swap(index(home, 1 - y, 3), "y")),
+    )
+    (layer_out,) = local_call(
+        finish_kernel, (shape(hidden, *hidden.shape),), (marks, hidden, *finals)
+    )
+    return (context_out, layer_out)
+
+
+def on_device(hidden, norm_gain, w_query, w_key, w_value, w_out):
+    rows, cols = lax.axis_size("row"), lax.axis_size("col")
+    heads_here = w_query.shape[1] // HD
+    paired = rows == 2**3 and cols == 2**2 and heads_here == rows and hidden.shape[0] % 64 == 0
+    plan = on_device_paired if paired else on_device_any
+    return plan(hidden, norm_gain, w_query, w_key, w_value, w_out)
 
 
 def solution(mesh):

time: 797 us -> 340 us (0.43)
  waiting for transfers between devices: 536 us -> 199 us
  blocking collectives: 161 us -> 0 us
  starting transfers between devices: 0.43 us -> 54.9 us
  Pallas kernels: 0 us -> 46.1 us
  matrix products: 42.8 us -> 0 us
  between operations: 14.2 us -> 1.59 us
    reduce_scatter x2 -> x0, waiting for transfers between devices: 350 us -> none  [the longest x1 205 us: on_device(): lax.psum_scatter(jnp.dot(segment, joined, preferred_element_type=jnp.floa...]
    ppermute x0 -> x55, waiting for transfers between devices: none -> 199 us  [swap(): return lax.ppermute(values, ('row', 'col'), pairs)]
    all_gather x4 -> x0, waiting for transfers between devices: 185 us -> none  [the longest x1 71.7 us: on_device(): lax.all_gather(keys_here, 'row', axis=0, tiled=True)]
    all_to_all x2 -> x0, blocking collectives: 153 us -> none  [the longest x1 98.9 us: on_device(): lax.all_to_all(normed, 'row', split_axis=1, concat_axis=0, tiled=True)]
    ppermute x0 -> x55, starting transfers between devices: none -> 54.9 us  [swap(): return lax.ppermute(values, ('row', 'col'), pairs)]
    pallas_call x0 -> x17, Pallas kernels: none -> 46.1 us  [local_call(): pl.pallas_call(kernel, name=getattr(kernel, '__name__', 'corners_kernel')...]
    dot_general x4 -> x0, matrix products: 42.8 us -> none  [the longest x1 18.5 us: on_device(): jnp.dot(segment, joined, preferred_element_type=jnp.float32)]
    add x1 -> x17, other arithmetic: 0.01 us -> 8.63 us  [the longest x10 6.23 us: on_device_paired(): total = keep + swap(send, 'y').astype(jnp.float32)]
  transfers between devices with their start and end apart: 6 -> 55, of which waited for: 6 -> 33; matrix products, arithmetic and copies ran while one was open for 2% -> 7% of each run, Pallas kernels for 0% -> 13%
where the time goes in v3:
time: 340 us; the launch traced here: 339 us
  waiting for transfers between devices  199 us (59%)
  starting transfers between devices  54.9 us (16%)
  Pallas kernels  46.1 us (14%)
  other arithmetic  19.8 us (6%)
  local copies, waits for them, and re-layouts  17.9 us (5%)
    ppermute x55, waiting for transfers between devices, swap(): return lax.ppermute(values, ('row', 'col'), pairs)  199 us
    ppermute x55, starting transfers between devices, swap(): return lax.ppermute(values, ('row', 'col'), pairs)  54.9 us
    pallas_call x17, Pallas kernels, local_call(): pl.pallas_call(kernel, name=getattr(kernel, '__name__', 'corners_kernel')...  46.1 us
    unnamed x85, local copies, waits for them, and re-layouts  14 us
  transfers between devices with their start and end apart: 55, of which 33 were waited for; matrix products, arithmetic and copies ran while one was open for 7% of the time, Pallas kernels for 13%

profile of v3, /device:TPU:0, one launch (start us, length us, event | category | flops | bytes accessed | tf_op | source)
XLA Modules:
  0.0 339.0 jit_solution(3297386321782142041)
XLA Ops:
  18.8 5.8 %collective-permute-done.3 = bf16[128,1024]{1,0:T(8,128)(2,1)} collective-permute-done((bf16[128,1024]{1,0:T(8,128)(2,1)S(1)}, bf16[128,1024]{1,0:T(8,128)(2,1)}, u32[]{:S(2)}, u32[]{:S(2)}) %collective-permute-start.3) | collective-permute-done | bytes 262176 | tf_op jit(solution)/shard_map/ppermute | solution.py:347
  24.6 5.0 %collective-permute-done.4 = bf16[128,1024]{1,0:T(8,128)(2,1)} collective-permute-done((bf16[128,1024]{1,0:T(8,128)(2,1)S(1)}, bf16[128,1024]{1,0:T(8,128)(2,1)}, u32[]{:S(2)}, u32[]{:S(2)}) %collective-permute-start.4) | collective-permute-done | bytes 262176 | tf_op jit(solution)/shard_map/ppermute | solution.py:347
  51.9 19.5 %collective-permute-done.8.refs_2_ = bf16[512,1024]{1,0:T(8,128)(2,1)} collective-permute-done((bf16[512,1024]{1,0:T(8,128)(2,1)S(1)}, bf16[512,1024]{1,0:T(8,128)(2,1)}, u32[]{:S(2)}, u32[]{:S(2)}) %collective-permute-start.8) | collective-permute-done | bytes 1048608 | tf_op jit(solution)/shard_map/ppermute | solution.py:347
  71.5 10.3 %collective-permute-done.15 = bf16[256,1024]{1,0:T(8,128)(2,1)} collective-permute-done((bf16[256,1024]{1,0:T(8,128)(2,1)S(1)}, bf16[256,1024]{1,0:T(8,128)(2,1)}, u32[]{:S(2)}, u32[]{:S(2)}) %collective-permute-start.15) | collective-permute-done | bytes 524320 | tf_op jit(solution)/shard_map/ppermute | solution.py:347
  81.8 5.3 %collective-permute-start.16 = (bf16[256,1024]{1,0:T(8,128)(2,1)}, bf16[256,1024]{1,0:T(8,128)(2,1)}, u32[]{:S(2)}, u32[]{:S(2)}) collective-permute-start(bf16[256,1024]{1,0:T(8,128)(2,1)} %collective-permute-done.15), channel_id=1, source_target_pairs={{0,8},{1,9},{2,10},{3,11},{4,12},{5,13},{6,14},{7,15},{8,0},{9,1},... | collective-permute-start | bytes 1572872 | tf_op jit(solution)/shard_map/ppermute | solution.py:347
  88.3 12.0 %collective-permute-done.16 = bf16[256,1024]{1,0:T(8,128)(2,1)} collective-permute-done((bf16[256,1024]{1,0:T(8,128)(2,1)}, bf16[256,1024]{1,0:T(8,128)(2,1)}, u32[]{:S(2)}, u32[]{:S(2)}) %collective-permute-start.16) | collective-permute-done | bytes 524320 | tf_op jit(solution)/shard_map/ppermute | solution.py:347
  122.1 5.0 %project_kernel.8 = (bf16[1024,256]{1,0:T(8,128)(2,1)S(1)}, f32[1024,256]{1,0:T(8,128)S(1)}) custom-call(s32[5]{0:T(128)S(1)} %stack.77.marks, bf16[512,1024]{1,0:T(8,128)(2,1)S(1)} %pad_maximum_fusion.2.refs_0_, bf16[512,1024]{1,0:T(8,128)(2,1)} %collective-permute-done.7.refs_1_, bf16[512,1024]{1,0:T(8,128)(2,1)} %collective-permute-done.8.refs_2_, ...), custom_call_target="tpu_custom_call" | custom-call | flops 1 | bytes 1 | tf_op jit(solution)/shard_map/project_kernel/pallas_call | solution.py:186
  128.6 6.5 %collective-permute-done.14 = bf16[1024,256]{1,0:T(8,128)(2,1)S(1)} collective-permute-done((bf16[1024,256]{1,0:T(8,128)(2,1)S(1)}, bf16[1024,256]{1,0:T(8,128)(2,1)S(1)}, u32[]{:S(2)}, u32[]{:S(2)}) %collective-permute-start.14) | collective-permute-done | bytes 524320 | tf_op jit(solution)/shard_map/ppermute | solution.py:347
  137.0 12.0 %collective-permute-done.13 = bf16[1024,128]{1,0:T(8,128)(2,1)S(1)} collective-permute-done((bf16[1024,128]{1,0:T(8,128)(2,1)S(1)}, bf16[1024,128]{1,0:T(8,128)(2,1)S(1)}, u32[]{:S(2)}, u32[]{:S(2)}) %collective-permute-start.13) | collective-permute-done | bytes 262176 | tf_op jit(solution)/shard_map/ppermute | solution.py:347
  162.8 5.2 %collective-permute-done.26 = bf16[1024,128]{1,0:T(8,128)(2,1)} collective-permute-done((bf16[1024,128]{1,0:T(8,128)(2,1)}, bf16[1024,128]{1,0:T(8,128)(2,1)}, u32[]{:S(2)}, u32[]{:S(2)}) %collective-permute-start.26) | collective-permute-done | bytes 262176 | tf_op jit(solution)/shard_map/ppermute | solution.py:347
  181.5 13.2 %collective-permute-done.28 = bf16[1024,128]{1,0:T(8,128)(2,1)S(1)} collective-permute-done((bf16[1024,128]{1,0:T(8,128)(2,1)S(1)}, bf16[1024,128]{1,0:T(8,128)(2,1)S(1)}, u32[]{:S(2)}, u32[]{:S(2)}) %collective-permute-start.28) | collective-permute-done | bytes 262176 | tf_op jit(solution)/shard_map/ppermute | solution.py:347
  199.9 8.9 %collective-permute-done.25 = bf16[1024,128]{1,0:T(8,128)(2,1)S(1)} collective-permute-done((bf16[1024,128]{1,0:T(8,128)(2,1)S(1)}, bf16[1024,128]{1,0:T(8,128)(2,1)S(1)}, u32[]{:S(2)}, u32[]{:S(2)}) %collective-permute-start.25) | collective-permute-done | bytes 262176 | tf_op jit(solution)/shard_map/ppermute | solution.py:347
  208.9 5.4 %attention_kernel.1 = bf16[4,8,64,128]{3,2,1,0:T(8,128)(2,1)S(1)} custom-call(s32[5]{0:T(128)S(1)} %stack.77.marks, f32[16,128,128]{2,1,0:T(8,128)S(1)} %bitcast.61, f32[16,128,128]{2,1,0:T(8,128)S(1)} %bitcast.59, f32[16,128,128]{2,1,0:T(8,128)S(1)} %bitcast.60, f32[2048,128]{1,0:T(8,128)S(1)} %copy-done.15, f32[2048,128]{1,0:T(8,128)S(1)} %copy-done.16), custom_call_target="tpu_custom_call" | custom-call | flops 1 | bytes 1 | tf_op jit(solution)/shard_map/attention_kernel/pallas_call | solution.py:186
  217.5 4.4 %collective-permute-done.35 = bf16[8,64,128]{2,1,0:T(8,128)(2,1)S(1)} collective-permute-done((bf16[8,64,128]{2,1,0:T(8,128)(2,1)S(1)}, bf16[8,64,128]{2,1,0:T(8,128)(2,1)S(1)}, u32[]{:S(2)}, u32[]{:S(2)}) %collective-permute-start.35) | collective-permute-done | bytes 131104 | tf_op jit(solution)/shard_map/ppermute | solution.py:347
  223.5 6.5 %collective-permute-done.31 = bf16[8,64,128]{2,1,0:T(8,128)(2,1)S(1)} collective-permute-done((bf16[8,64,128]{2,1,0:T(8,128)(2,1)S(1)}, bf16[8,64,128]{2,1,0:T(8,128)(2,1)S(1)}, u32[]{:S(2)}, u32[]{:S(2)}) %collective-permute-start.31) | collective-permute-done | bytes 131104 | tf_op jit(solution)/shard_map/ppermute | solution.py:347
  230.3 7.5 %collective-permute-done.32 = bf16[2,8,64,128]{3,2,1,0:T(8,128)(2,1)S(1)} collective-permute-done((bf16[2,8,64,128]{3,2,1,0:T(8,128)(2,1)S(1)}, bf16[2,8,64,128]{3,2,1,0:T(8,128)(2,1)S(1)}, u32[]{:S(2)}, u32[]{:S(2)}) %collective-permute-start.32) | collective-permute-done | bytes 262176 | tf_op jit(solution)/shard_map/ppermute | solution.py:347
  238.5 7.1 %collective-permute-done.36 = bf16[8,64,128]{2,1,0:T(8,128)(2,1)S(1)} collective-permute-done((bf16[8,64,128]{2,1,0:T(8,128)(2,1)S(1)}, bf16[8,64,128]{2,1,0:T(8,128)(2,1)S(1)}, u32[]{:S(2)}, u32[]{:S(2)}) %collective-permute-start.36) | collective-permute-done | bytes 131104 | tf_op jit(solution)/shard_map/ppermute | solution.py:347
  245.8 6.5 %collective-permute-done.37 = bf16[2,8,64,128]{3,2,1,0:T(8,128)(2,1)S(1)} collective-permute-done((bf16[2,8,64,128]{3,2,1,0:T(8,128)(2,1)S(1)}, bf16[2,8,64,128]{3,2,1,0:T(8,128)(2,1)S(1)}, u32[]{:S(2)}, u32[]{:S(2)}) %collective-permute-start.37) | collective-permute-done | bytes 262176 | tf_op jit(solution)/shard_map/ppermute | solution.py:347
  267.0 9.3 %collective-permute-done.39 = bf16[4,2,2,64,128]{4,3,2,1,0:T(8,128)(2,1)S(1)} collective-permute-done((bf16[4,2,2,64,128]{4,3,2,1,0:T(8,128)(2,1)}, bf16[4,2,2,64,128]{4,3,2,1,0:T(8,128)(2,1)S(1)}, u32[]{:S(2)}, u32[]{:S(2)}) %collective-permute-start.39) | collective-permute-done | bytes 262176 | tf_op jit(solution)/shard_map/ppermute | solution.py:347
  280.1 5.9 %collective-permute-done.44 = bf16[512,512]{1,0:T(8,128)(2,1)} collective-permute-done((bf16[512,512]{1,0:T(8,128)(2,1)}, bf16[512,512]{1,0:T(8,128)(2,1)}, u32[]{:S(2)}, u32[]{:S(2)}) %collective-permute-start.44) | collective-permute-done | bytes 524320 | tf_op jit(solution)/shard_map/ppermute | solution.py:347
  292.2 7.3 %collective-permute-done.46 = bf16[256,512]{1,0:T(8,128)(2,1)S(1)} collective-permute-done((bf16[256,512]{1,0:T(8,128)(2,1)S(1)}, bf16[256,512]{1,0:T(8,128)(2,1)S(1)}, u32[]{:S(2)}, u32[]{:S(2)}) %collective-permute-start.46) | collective-permute-done | bytes 262176 | tf_op jit(solution)/shard_map/ppermute | solution.py:347
  309.3 6.4 %collective-permute-done.47 = bf16[512,512]{1,0:T(8,128)(2,1)S(1)} collective-permute-done((bf16[512,512]{1,0:T(8,128)(2,1)S(1)}, bf16[512,512]{1,0:T(8,128)(2,1)S(1)}, u32[]{:S(2)}, u32[]{:S(2)}) %collective-permute-start.47) | collective-permute-done | bytes 524320 | tf_op jit(solution)/shard_map/ppermute | solution.py:347
  319.5 6.0 %collective-permute-done.52 = bf16[256,512]{1,0:T(8,128)(2,1)S(1)} collective-permute-done((bf16[256,512]{1,0:T(8,128)(2,1)S(1)}, bf16[256,512]{1,0:T(8,128)(2,1)S(1)}, u32[]{:S(2)}, u32[]{:S(2)}) %collective-permute-start.52) | collective-permute-done | bytes 262176 | tf_op jit(solution)/shard_map/ppermute | solution.py:347
  331.7 5.6 %collective-permute-done.54.refs_3_ = bf16[128,1024]{1,0:T(8,128)(2,1)S(1)} collective-permute-done((bf16[128,1024]{1,0:T(8,128)(2,1)S(1)}, bf16[128,1024]{1,0:T(8,128)(2,1)S(1)}, u32[]{:S(2)}, u32[]{:S(2)}) %collective-permute-start.54) | collective-permute-done | bytes 262176 | tf_op jit(solution)/shard_map/ppermute | solution.py:347
  (255 shorter events, 150.8 us)
Async XLA Ops:
  6.0 26.5 %collective-permute-start.5 = (bf16[1024,512]{1,0:T(8,128)(2,1)S(1)}, bf16[1024,512]{1,0:T(8,128)(2,1)S(1)}, u32[]{:S(2)}, u32[]{:S(2)}) collective-permute-start(bf16[1024,512]{1,0:T(8,128)(2,1)S(1)} %get-tuple-element.73), channel_id=1, source_target_pairs={{0,8},{1,9},{2,10},{3,11},{4,12},{5,13},{6,14},{7,15},{8,0},{9,1},... | collective-permute-start | bytes 3145736 | tf_op jit(solution)/shard_map/ppermute | solution.py:347
  46.8 24.7 %collective-permute-start.8 = (bf16[512,1024]{1,0:T(8,128)(2,1)S(1)}, bf16[512,1024]{1,0:T(8,128)(2,1)}, u32[]{:S(2)}, u32[]{:S(2)}) collective-permute-start(bf16[512,1024]{1,0:T(8,128)(2,1)S(1)} %pad_maximum_fusion.2.refs_0_), channel_id=1, source_target_pairs={{0,2},{1,3},{2,0},{3,1},{4,6},{5,7},{6,4},{7,5},{8,10},{9,11},{10,... | collective-permute-start | bytes 3145736 | tf_op jit(solution)/shard_map/ppermute | solution.py:347
  48.4 39.8 %collective-permute-start.10 = (bf16[1024,512]{1,0:T(8,128)(2,1)S(1)}, bf16[1024,512]{1,0:T(8,128)(2,1)}, u32[]{:S(2)}, u32[]{:S(2)}) collective-permute-start(bf16[1024,512]{1,0:T(8,128)(2,1)S(1)} %get-tuple-element.91), channel_id=1, source_target_pairs={{0,8},{1,9},{2,10},{3,11},{4,12},{5,13},{6,14},{7,15},{8,0},{9,1},... | collective-permute-start | bytes 3145736 | tf_op jit(solution)/shard_map/ppermute | solution.py:347
  49.4 32.4 %collective-permute-start.15 = (bf16[256,1024]{1,0:T(8,128)(2,1)S(1)}, bf16[256,1024]{1,0:T(8,128)(2,1)}, u32[]{:S(2)}, u32[]{:S(2)}) collective-permute-start(bf16[256,1024]{1,0:T(8,128)(2,1)S(1)} %get-tuple-element.103), channel_id=1, source_target_pairs={{0,16},{1,17},{2,18},{3,19},{4,20},{5,21},{6,22},{7,23},{8,24},{9,... | collective-permute-start | bytes 1572872 | tf_op jit(solution)/shard_map/ppermute | solution.py:347
  51.9 51.6 %collective-permute-start.7 = (bf16[512,1024]{1,0:T(8,128)(2,1)S(1)}, bf16[512,1024]{1,0:T(8,128)(2,1)}, u32[]{:S(2)}, u32[]{:S(2)}) collective-permute-start(bf16[512,1024]{1,0:T(8,128)(2,1)S(1)} %pad_maximum_fusion.2.refs_0_), channel_id=1, source_target_pairs={{0,1},{1,0},{2,3},{3,2},{4,5},{5,4},{6,7},{7,6},{8,9},{9,8},{10,11... | collective-permute-start | bytes 3145736 | tf_op jit(solution)/shard_map/ppermute | solution.py:347
  71.5 32.0 %collective-permute-start.9 = (bf16[512,1024]{1,0:T(8,128)(2,1)}, bf16[512,1024]{1,0:T(8,128)(2,1)}, u32[]{:S(2)}, u32[]{:S(2)}) collective-permute-start(bf16[512,1024]{1,0:T(8,128)(2,1)} %collective-permute-done.8.refs_2_), channel_id=1, source_target_pairs={{0,1},{1,0},{2,3},{3,2},{4,5},{5,4},{6,7},{7,6},{8,9},{9,8},{10,11... | collective-permute-start | bytes 3145736 | tf_op jit(solution)/shard_map/ppermute | solution.py:347
  81.8 18.4 %collective-permute-start.16 = (bf16[256,1024]{1,0:T(8,128)(2,1)}, bf16[256,1024]{1,0:T(8,128)(2,1)}, u32[]{:S(2)}, u32[]{:S(2)}) collective-permute-start(bf16[256,1024]{1,0:T(8,128)(2,1)} %collective-permute-done.15), channel_id=1, source_target_pairs={{0,8},{1,9},{2,10},{3,11},{4,12},{5,13},{6,14},{7,15},{8,0},{9,1},... | collective-permute-start | bytes 1572872 | tf_op jit(solution)/shard_map/ppermute | solution.py:347
  88.2 33.7 %collective-permute-start.12 = (bf16[1024,512]{1,0:T(8,128)(2,1)}, bf16[1024,512]{1,0:T(8,128)(2,1)S(1)}, u32[]{:S(2)}, u32[]{:S(2)}) collective-permute-start(bf16[1024,512]{1,0:T(8,128)(2,1)} %get-tuple-element.96), channel_id=1, source_target_pairs={{0,8},{1,9},{2,10},{3,11},{4,12},{5,13},{6,14},{7,15},{8,0},{9,1},... | collective-permute-start | bytes 3145736 | tf_op jit(solution)/shard_map/ppermute | solution.py:347
  101.3 19.1 %collective-permute-start.18 = (bf16[512,1024]{1,0:T(8,128)(2,1)S(1)}, bf16[512,1024]{1,0:T(8,128)(2,1)S(1)}, u32[]{:S(2)}, u32[]{:S(2)}) collective-permute-start(bf16[512,1024]{1,0:T(8,128)(2,1)S(1)} %constant_dynamic-update-slice_fusion.refs_0_), channel_id=1, source_target_pairs={{0,2},{1,3},{2,0},{3,1},{4,6},{5,7},{6,4},{7,5},{8,10},{9,11},{10,... | collective-permute-start | bytes 3145736 | tf_op jit(solution)/shard_map/ppermute | solution.py:347
  109.5 39.4 %collective-permute-start.17 = (bf16[512,1024]{1,0:T(8,128)(2,1)S(1)}, bf16[512,1024]{1,0:T(8,128)(2,1)S(1)}, u32[]{:S(2)}, u32[]{:S(2)}) collective-permute-start(bf16[512,1024]{1,0:T(8,128)(2,1)S(1)} %constant_dynamic-update-slice_fusion.refs_0_), channel_id=1, source_target_pairs={{0,1},{1,0},{2,3},{3,2},{4,5},{5,4},{6,7},{7,6},{8,9},{9,8},{10,11... | collective-permute-start | bytes 3145736 | tf_op jit(solution)/shard_map/ppermute | solution.py:347
  120.4 28.6 %collective-permute-start.19 = (bf16[512,1024]{1,0:T(8,128)(2,1)S(1)}, bf16[512,1024]{1,0:T(8,128)(2,1)S(1)}, u32[]{:S(2)}, u32[]{:S(2)}) collective-permute-start(bf16[512,1024]{1,0:T(8,128)(2,1)S(1)} %collective-permute-done.18.refs_2_), channel_id=1, source_target_pairs={{0,1},{1,0},{2,3},{3,2},{4,5},{5,4},{6,7},{7,6},{8,9},{9,8},{10,11... | collective-permute-start | bytes 3145736 | tf_op jit(solution)/shard_map/ppermute | solution.py:347
  127.1 28.1 %collective-permute-start.20 = (bf16[1024,256]{1,0:T(8,128)(2,1)S(1)}, bf16[1024,256]{1,0:T(8,128)(2,1)S(1)}, u32[]{:S(2)}, u32[]{:S(2)}) collective-permute-start(bf16[1024,256]{1,0:T(8,128)(2,1)S(1)} %get-tuple-element.108), channel_id=1, source_target_pairs={{0,4},{1,5},{2,6},{3,7},{4,0},{5,1},{6,2},{7,3},{8,12},{9,13},{10,... | collective-permute-start | bytes 1572872 | tf_op jit(solution)/shard_map/ppermute | solution.py:347
  127.7 21.3 %collective-permute-start.13 = (bf16[1024,128]{1,0:T(8,128)(2,1)S(1)}, bf16[1024,128]{1,0:T(8,128)(2,1)S(1)}, u32[]{:S(2)}, u32[]{:S(2)}) collective-permute-start(bf16[1024,128]{1,0:T(8,128)(2,1)S(1)} %slice.207), channel_id=1, source_target_pairs={{0,16},{1,17},{2,18},{3,19},{4,20},{5,21},{6,22},{7,23},{8,24},{9,... | collective-permute-start | bytes 786440 | tf_op jit(solution)/shard_map/ppermute | solution.py:347
  136.0 26.7 %collective-permute-start.21 = (bf16[1024,128]{1,0:T(8,128)(2,1)}, bf16[1024,128]{1,0:T(8,128)(2,1)}, u32[]{:S(2)}, u32[]{:S(2)}) collective-permute-start(bf16[1024,128]{1,0:T(8,128)(2,1)} %slice.206), channel_id=1, source_target_pairs={{0,16},{1,17},{2,18},{3,19},{4,20},{5,21},{6,22},{7,23},{8,24},{9,... | collective-permute-start | bytes 786440 | tf_op jit(solution)/shard_map/ppermute | solution.py:347
  160.8 17.0 %collective-permute-start.27 = (bf16[1024,256]{1,0:T(8,128)(2,1)}, bf16[1024,256]{1,0:T(8,128)(2,1)}, u32[]{:S(2)}, u32[]{:S(2)}) collective-permute-start(bf16[1024,256]{1,0:T(8,128)(2,1)} %get-tuple-element.123), channel_id=1, source_target_pairs={{0,4},{1,5},{2,6},{3,7},{4,0},{5,1},{6,2},{7,3},{8,12},{9,13},{10,... | collective-permute-start | bytes 1572872 | tf_op jit(solution)/shard_map/ppermute | solution.py:347
  161.3 53.0 %collective-permute-start.29 = (bf16[512,1024]{1,0:T(8,128)(2,1)}, bf16[512,1024]{1,0:T(8,128)(2,1)S(1)}, u32[]{:S(2)}, u32[]{:S(2)}) collective-permute-start(bf16[512,1024]{1,0:T(8,128)(2,1)} %copy-done.32), channel_id=1, source_target_pairs={{0,8},{1,9},{2,10},{3,11},{4,12},{5,13},{6,14},{7,15},{8,0},{9,1},... | collective-permute-start | bytes 3145736 | tf_op jit(solution)/shard_map/ppermute | solution.py:347
  170.3 24.4 %collective-permute-start.23 = (bf16[1024,128]{1,0:T(8,128)(2,1)S(1)}, bf16[1024,128]{1,0:T(8,128)(2,1)S(1)}, u32[]{:S(2)}, u32[]{:S(2)}) collective-permute-start(bf16[1024,128]{1,0:T(8,128)(2,1)S(1)} %slice.204), channel_id=1, source_target_pairs={{0,16},{1,17},{2,18},{3,19},{4,20},{5,21},{6,22},{7,23},{8,24},{9,... | collective-permute-start | bytes 786440 | tf_op jit(solution)/shard_map/ppermute | solution.py:347
  174.6 20.4 %collective-permute-start.24 = (bf16[1024,256]{1,0:T(8,128)(2,1)S(1)}, bf16[1024,256]{1,0:T(8,128)(2,1)S(1)}, u32[]{:S(2)}, u32[]{:S(2)}) collective-permute-start(bf16[1024,256]{1,0:T(8,128)(2,1)S(1)} %get-tuple-element.119), channel_id=1, source_target_pairs={{0,4},{1,5},{2,6},{3,7},{4,0},{5,1},{6,2},{7,3},{8,12},{9,13},{10,... | collective-permute-start | bytes 1572872 | tf_op jit(solution)/shard_map/ppermute | solution.py:347
  262.1 23.9 %collective-permute-start.44 = (bf16[512,512]{1,0:T(8,128)(2,1)}, bf16[512,512]{1,0:T(8,128)(2,1)}, u32[]{:S(2)}, u32[]{:S(2)}) collective-permute-start(bf16[512,512]{1,0:T(8,128)(2,1)} %copy-done.33), channel_id=1, source_target_pairs={{0,4},{1,5},{2,6},{3,7},{4,0},{5,1},{6,2},{7,3},{8,12},{9,13},{10,... | collective-permute-start | bytes 1572872 | tf_op jit(solution)/shard_map/ppermute | solution.py:347
  263.2 24.2 %collective-permute-start.42 = (bf16[2,2,8,64,128]{4,3,2,1,0:T(8,128)(2,1)S(1)}, bf16[2,2,8,64,128]{4,3,2,1,0:T(8,128)(2,1)S(1)}, u32[]{:S(2)}, u32[]{:S(2)}) collective-permute-start(bf16[2,2,8,64,128]{4,3,2,1,0:T(8,128)(2,1)S(1)} %pad_maximum_fusion.11.own_0), channel_id=1, source_target_pairs={{0,1},{1,0},{2,3},{3,2},{4,5},{5,4},{6,7},{7,6},{8,9},{9,8},{10,11... | collective-permute-start | bytes 1572872 | tf_op jit(solution)/shard_map/ppermute | solution.py:347
  267.0 20.4 %collective-permute-start.43 = (bf16[2,2,8,64,128]{4,3,2,1,0:T(8,128)(2,1)}, bf16[2,2,8,64,128]{4,3,2,1,0:T(8,128)(2,1)S(1)}, u32[]{:S(2)}, u32[]{:S(2)}) collective-permute-start(bf16[2,2,8,64,128]{4,3,2,1,0:T(8,128)(2,1)} %collective-permute-done.41.own_1), channel_id=1, source_target_pairs={{0,1},{1,0},{2,3},{3,2},{4,5},{5,4},{6,7},{7,6},{8,9},{9,8},{10,11... | collective-permute-start | bytes 1572872 | tf_op jit(solution)/shard_map/ppermute | solution.py:347
  278.1 21.4 %collective-permute-start.46 = (bf16[256,512]{1,0:T(8,128)(2,1)S(1)}, bf16[256,512]{1,0:T(8,128)(2,1)S(1)}, u32[]{:S(2)}, u32[]{:S(2)}) collective-permute-start(bf16[256,512]{1,0:T(8,128)(2,1)S(1)} %slice.200), channel_id=1, source_target_pairs={{0,16},{1,17},{2,18},{3,19},{4,20},{5,21},{6,22},{7,23},{8,24},{9,... | collective-permute-start | bytes 786440 | tf_op jit(solution)/shard_map/ppermute | solution.py:347
  304.3 27.4 %collective-permute-start.50 = (bf16[128,1024]{1,0:T(8,128)(2,1)S(1)}, bf16[128,1024]{1,0:T(8,128)(2,1)S(1)}, u32[]{:S(2)}, u32[]{:S(2)}) collective-permute-start(bf16[128,1024]{1,0:T(8,128)(2,1)S(1)} %pad_maximum_fusion.15), channel_id=1, source_target_pairs={{0,8},{1,9},{2,10},{3,11},{4,12},{5,13},{6,14},{7,15},{8,0},{9,1},... | collective-permute-start | bytes 786440 | tf_op jit(solution)/shard_map/ppermute | solution.py:347
  306.3 19.1 %collective-permute-start.52 = (bf16[256,512]{1,0:T(8,128)(2,1)S(1)}, bf16[256,512]{1,0:T(8,128)(2,1)S(1)}, u32[]{:S(2)}, u32[]{:S(2)}) collective-permute-start(bf16[256,512]{1,0:T(8,128)(2,1)S(1)} %slice.198), channel_id=1, source_target_pairs={{0,16},{1,17},{2,18},{3,19},{4,20},{5,21},{6,22},{7,23},{8,24},{9,... | collective-permute-start | bytes 786440 | tf_op jit(solution)/shard_map/ppermute | solution.py:347
  (73 other events, 660.7 us)

commit v4 on v3

--- a/solution.py
+++ b/solution.py
@@ -415,14 +415,14 @@
     for i in range(6):
         if i == 1:
             products.append(multiply(pairs_a, *weights[2], sums[0]))
-            beside_b = after(beside_b, sums[0])
+            beside_b = after(beside_b, products[1][0])
             pairs_b = ((held_b, core_b), (beside_b, swap(beside_b, "core")))
         if 2 <= i < 5:
             products.append(multiply(pairs_b, *weights[i - 2], sums[i - 1]))
         send, keep = products[i]
         if i >= 2:
             send = after(send, sums[i - 2])
-            keep = after(keep, got[i - 2])
+            keep = after(keep, *(got[i - 2 : i - 1] if i >= 3 else ()))
         if i < 5:
             keep = after(keep, products[i + 1][0])
         total = keep + swap(send, "y").astype(jnp.float32)
@@ -473,7 +473,7 @@
     for i, (send, keep) in enumerate(
         ((first[0], first[2]), (first[1], first[3]), (second[0], second[2]), (second[1], second[3]))
     ):
-        if i == 0:
+        if i == 1:
             keep = after(keep, home)
         if i == 3:
             home = jnp.stack((index(home, zl, 2), swap(index(home, 1 - zl, 2), "zl")))

time: 340 us -> 335 us (0.985)
    unnamed x85 -> x89, local copies, waits for them, and re-layouts: 14 us -> 14.4 us
where the time goes in v4:
time: 335 us; the launch traced here: 334 us
  waiting for transfers between devices  196 us (59%)
  starting transfers between devices  54.3 us (16%)
  Pallas kernels  45.5 us (14%)
  other arithmetic  18.9 us (6%)
  local copies, waits for them, and re-layouts  18.2 us (5%)
    ppermute x55, waiting for transfers between devices, swap(): return lax.ppermute(values, ('row', 'col'), pairs)  196 us
    ppermute x55, starting transfers between devices, swap(): return lax.ppermute(values, ('row', 'col'), pairs)  54.3 us
    pallas_call x17, Pallas kernels, local_call(): pl.pallas_call(kernel, name=getattr(kernel, '__name__', 'corners_kernel')...  45.5 us
    unnamed x89, local copies, waits for them, and re-layouts  14.4 us
  transfers between devices with their start and end apart: 55, of which 33 were waited for; matrix products, arithmetic and copies ran while one was open for 7% of the time, Pallas kernels for 13%

profile of v4, /device:TPU:0, one launch (start us, length us, event | category | flops | bytes accessed | tf_op | source)
XLA Modules:
  0.0 334.5 jit_solution(1430900046568642538)
XLA Ops:
  18.8 5.8 %collective-permute-done.3 = bf16[128,1024]{1,0:T(8,128)(2,1)} collective-permute-done((bf16[128,1024]{1,0:T(8,128)(2,1)S(1)}, bf16[128,1024]{1,0:T(8,128)(2,1)}, u32[]{:S(2)}, u32[]{:S(2)}) %collective-permute-start.3) | collective-permute-done | bytes 262176 | tf_op jit(solution)/shard_map/ppermute | solution.py:347
  24.6 5.0 %collective-permute-done.4 = bf16[128,1024]{1,0:T(8,128)(2,1)} collective-permute-done((bf16[128,1024]{1,0:T(8,128)(2,1)S(1)}, bf16[128,1024]{1,0:T(8,128)(2,1)}, u32[]{:S(2)}, u32[]{:S(2)}) %collective-permute-start.4) | collective-permute-done | bytes 262176 | tf_op jit(solution)/shard_map/ppermute | solution.py:347
  51.9 21.5 %collective-permute-done.14 = bf16[256,1024]{1,0:T(8,128)(2,1)S(1)} collective-permute-done((bf16[256,1024]{1,0:T(8,128)(2,1)S(1)}, bf16[256,1024]{1,0:T(8,128)(2,1)S(1)}, u32[]{:S(2)}, u32[]{:S(2)}) %collective-permute-start.14) | collective-permute-done | bytes 524320 | tf_op jit(solution)/shard_map/ppermute | solution.py:347
  74.0 23.2 %collective-permute-done.15 = bf16[256,1024]{1,0:T(8,128)(2,1)S(1)} collective-permute-done((bf16[256,1024]{1,0:T(8,128)(2,1)S(1)}, bf16[256,1024]{1,0:T(8,128)(2,1)S(1)}, u32[]{:S(2)}, u32[]{:S(2)}) %collective-permute-start.15) | collective-permute-done | bytes 524320 | tf_op jit(solution)/shard_map/ppermute | solution.py:347
  101.1 4.4 %project_kernel.6 = (bf16[1024,256]{1,0:T(8,128)(2,1)S(1)}, f32[1024,256]{1,0:T(8,128)S(1)}) custom-call(s32[5]{0:T(128)S(1)} %stack.77.marks, bf16[512,1024]{1,0:T(8,128)(2,1)S(1)} %pad_maximum_fusion.2.refs_0_, bf16[512,1024]{1,0:T(8,128)(2,1)} %collective-permute-done.7.refs_1_, bf16[512,1024]{1,0:T(8,128)(2,1)} %collective-permute-done.8.refs_2_, ...), custom_call_target="tpu_custom_call" | custom-call | flops 1 | bytes 1 | tf_op jit(solution)/shard_map/project_kernel/pallas_call | solution.py:186
  107.2 4.3 %project_kernel.7 = (bf16[1024,256]{1,0:T(8,128)(2,1)S(1)}, f32[1024,256]{1,0:T(8,128)S(1)}) custom-call(s32[5]{0:T(128)S(1)} %stack.77.marks, bf16[512,1024]{1,0:T(8,128)(2,1)S(1)} %pad_maximum_fusion.2.refs_0_, bf16[512,1024]{1,0:T(8,128)(2,1)} %collective-permute-done.7.refs_1_, bf16[512,1024]{1,0:T(8,128)(2,1)} %collective-permute-done.8.refs_2_, ...), custom_call_target="tpu_custom_call" | custom-call | flops 1 | bytes 1 | tf_op jit(solution)/shard_map/project_kernel/pallas_call | solution.py:186
  112.1 8.2 %collective-permute-done.17.refs_2_ = bf16[512,1024]{1,0:T(8,128)(2,1)S(1)} collective-permute-done((bf16[512,1024]{1,0:T(8,128)(2,1)S(1)}, bf16[512,1024]{1,0:T(8,128)(2,1)S(1)}, u32[]{:S(2)}, u32[]{:S(2)}) %collective-permute-start.17) | collective-permute-done | bytes 1048608 | tf_op jit(solution)/shard_map/ppermute | solution.py:347
  139.1 4.9 %collective-permute-done.19 = bf16[1024,256]{1,0:T(8,128)(2,1)S(1)} collective-permute-done((bf16[1024,256]{1,0:T(8,128)(2,1)S(1)}, bf16[1024,256]{1,0:T(8,128)(2,1)S(1)}, u32[]{:S(2)}, u32[]{:S(2)}) %collective-permute-start.19) | collective-permute-done | bytes 524320 | tf_op jit(solution)/shard_map/ppermute | solution.py:347
  171.7 10.1 %collective-permute-done.28 = bf16[1024,128]{1,0:T(8,128)(2,1)S(1)} collective-permute-done((bf16[1024,128]{1,0:T(8,128)(2,1)}, bf16[1024,128]{1,0:T(8,128)(2,1)S(1)}, u32[]{:S(2)}, u32[]{:S(2)}) %collective-permute-start.28) | collective-permute-done | bytes 262176 | tf_op jit(solution)/shard_map/ppermute | solution.py:347
  181.9 8.2 %collective-permute-done.27 = bf16[1024,128]{1,0:T(8,128)(2,1)S(1)} collective-permute-done((bf16[1024,128]{1,0:T(8,128)(2,1)S(1)}, bf16[1024,128]{1,0:T(8,128)(2,1)S(1)}, u32[]{:S(2)}, u32[]{:S(2)}) %collective-permute-start.27) | collective-permute-done | bytes 262176 | tf_op jit(solution)/shard_map/ppermute | solution.py:347
  194.2 9.9 %collective-permute-done.24 = bf16[1024,128]{1,0:T(8,128)(2,1)S(1)} collective-permute-done((bf16[1024,128]{1,0:T(8,128)(2,1)S(1)}, bf16[1024,128]{1,0:T(8,128)(2,1)S(1)}, u32[]{:S(2)}, u32[]{:S(2)}) %collective-permute-start.24) | collective-permute-done | bytes 262176 | tf_op jit(solution)/shard_map/ppermute | solution.py:347
  204.3 5.4 %attention_kernel.1 = bf16[4,8,64,128]{3,2,1,0:T(8,128)(2,1)S(1)} custom-call(s32[5]{0:T(128)S(1)} %stack.77.marks, f32[16,128,128]{2,1,0:T(8,128)S(1)} %bitcast.61, f32[16,128,128]{2,1,0:T(8,128)S(1)} %bitcast.59, f32[16,128,128]{2,1,0:T(8,128)S(1)} %bitcast.60, f32[2048,128]{1,0:T(8,128)S(1)} %copy-done.15, f32[2048,128]{1,0:T(8,128)S(1)} %copy-done.16), custom_call_target="tpu_custom_call" | custom-call | flops 1 | bytes 1 | tf_op jit(solution)/shard_map/attention_kernel/pallas_call | solution.py:186
  212.8 4.3 %collective-permute-done.35 = bf16[8,64,128]{2,1,0:T(8,128)(2,1)S(1)} collective-permute-done((bf16[8,64,128]{2,1,0:T(8,128)(2,1)S(1)}, bf16[8,64,128]{2,1,0:T(8,128)(2,1)S(1)}, u32[]{:S(2)}, u32[]{:S(2)}) %collective-permute-start.35) | collective-permute-done | bytes 131104 | tf_op jit(solution)/shard_map/ppermute | solution.py:347
  219.2 6.0 %collective-permute-done.31 = bf16[8,64,128]{2,1,0:T(8,128)(2,1)S(1)} collective-permute-done((bf16[8,64,128]{2,1,0:T(8,128)(2,1)S(1)}, bf16[8,64,128]{2,1,0:T(8,128)(2,1)S(1)}, u32[]{:S(2)}, u32[]{:S(2)}) %collective-permute-start.31) | collective-permute-done | bytes 131104 | tf_op jit(solution)/shard_map/ppermute | solution.py:347
  225.5 7.0 %collective-permute-done.32 = bf16[2,8,64,128]{3,2,1,0:T(8,128)(2,1)S(1)} collective-permute-done((bf16[2,8,64,128]{3,2,1,0:T(8,128)(2,1)S(1)}, bf16[2,8,64,128]{3,2,1,0:T(8,128)(2,1)S(1)}, u32[]{:S(2)}, u32[]{:S(2)}) %collective-permute-start.32) | collective-permute-done | bytes 262176 | tf_op jit(solution)/shard_map/ppermute | solution.py:347
  234.2 7.0 %collective-permute-done.36 = bf16[8,64,128]{2,1,0:T(8,128)(2,1)S(1)} collective-permute-done((bf16[8,64,128]{2,1,0:T(8,128)(2,1)S(1)}, bf16[8,64,128]{2,1,0:T(8,128)(2,1)S(1)}, u32[]{:S(2)}, u32[]{:S(2)}) %collective-permute-start.36) | collective-permute-done | bytes 131104 | tf_op jit(solution)/shard_map/ppermute | solution.py:347
  241.4 6.3 %collective-permute-done.37 = bf16[2,8,64,128]{3,2,1,0:T(8,128)(2,1)S(1)} collective-permute-done((bf16[2,8,64,128]{3,2,1,0:T(8,128)(2,1)S(1)}, bf16[2,8,64,128]{3,2,1,0:T(8,128)(2,1)S(1)}, u32[]{:S(2)}, u32[]{:S(2)}) %collective-permute-start.37) | collective-permute-done | bytes 262176 | tf_op jit(solution)/shard_map/ppermute | solution.py:347
  262.2 8.9 %collective-permute-done.39 = bf16[4,2,2,64,128]{4,3,2,1,0:T(8,128)(2,1)S(1)} collective-permute-done((bf16[4,2,2,64,128]{4,3,2,1,0:T(8,128)(2,1)}, bf16[4,2,2,64,128]{4,3,2,1,0:T(8,128)(2,1)S(1)}, u32[]{:S(2)}, u32[]{:S(2)}) %collective-permute-start.39) | collective-permute-done | bytes 262176 | tf_op jit(solution)/shard_map/ppermute | solution.py:347
  275.2 5.9 %collective-permute-done.44 = bf16[512,512]{1,0:T(8,128)(2,1)} collective-permute-done((bf16[512,512]{1,0:T(8,128)(2,1)}, bf16[512,512]{1,0:T(8,128)(2,1)}, u32[]{:S(2)}, u32[]{:S(2)}) %collective-permute-start.44) | collective-permute-done | bytes 524320 | tf_op jit(solution)/shard_map/ppermute | solution.py:347
  288.0 6.4 %collective-permute-done.46 = bf16[256,512]{1,0:T(8,128)(2,1)S(1)} collective-permute-done((bf16[256,512]{1,0:T(8,128)(2,1)S(1)}, bf16[256,512]{1,0:T(8,128)(2,1)S(1)}, u32[]{:S(2)}, u32[]{:S(2)}) %collective-permute-start.46) | collective-permute-done | bytes 262176 | tf_op jit(solution)/shard_map/ppermute | solution.py:347
  304.5 6.3 %collective-permute-done.47 = bf16[512,512]{1,0:T(8,128)(2,1)S(1)} collective-permute-done((bf16[512,512]{1,0:T(8,128)(2,1)S(1)}, bf16[512,512]{1,0:T(8,128)(2,1)S(1)}, u32[]{:S(2)}, u32[]{:S(2)}) %collective-permute-start.47) | collective-permute-done | bytes 524320 | tf_op jit(solution)/shard_map/ppermute | solution.py:347
  314.3 6.3 %collective-permute-done.52 = bf16[256,512]{1,0:T(8,128)(2,1)S(1)} collective-permute-done((bf16[256,512]{1,0:T(8,128)(2,1)S(1)}, bf16[256,512]{1,0:T(8,128)(2,1)S(1)}, u32[]{:S(2)}, u32[]{:S(2)}) %collective-permute-start.52) | collective-permute-done | bytes 262176 | tf_op jit(solution)/shard_map/ppermute | solution.py:347
  320.7 4.5 %collective-permute-done.53 = bf16[256,512]{1,0:T(8,128)(2,1)S(1)} collective-permute-done((bf16[256,512]{1,0:T(8,128)(2,1)S(1)}, bf16[256,512]{1,0:T(8,128)(2,1)S(1)}, u32[]{:S(2)}, u32[]{:S(2)}) %collective-permute-start.53) | collective-permute-done | bytes 262176 | tf_op jit(solution)/shard_map/ppermute | solution.py:347
  327.0 5.8 %collective-permute-done.54.refs_3_ = bf16[128,1024]{1,0:T(8,128)(2,1)S(1)} collective-permute-done((bf16[128,1024]{1,0:T(8,128)(2,1)S(1)}, bf16[128,1024]{1,0:T(8,128)(2,1)S(1)}, u32[]{:S(2)}, u32[]{:S(2)}) %collective-permute-start.54) | collective-permute-done | bytes 262176 | tf_op jit(solution)/shard_map/ppermute | solution.py:347
  (259 shorter events, 146.9 us)
Async XLA Ops:
  6.0 26.5 %collective-permute-start.5 = (bf16[1024,512]{1,0:T(8,128)(2,1)S(1)}, bf16[1024,512]{1,0:T(8,128)(2,1)S(1)}, u32[]{:S(2)}, u32[]{:S(2)}) collective-permute-start(bf16[1024,512]{1,0:T(8,128)(2,1)S(1)} %get-tuple-element.72), channel_id=1, source_target_pairs={{0,8},{1,9},{2,10},{3,11},{4,12},{5,13},{6,14},{7,15},{8,0},{9,1},... | collective-permute-start | bytes 3145736 | tf_op jit(solution)/shard_map/ppermute | solution.py:347
  46.8 26.7 %collective-permute-start.8 = (bf16[512,1024]{1,0:T(8,128)(2,1)S(1)}, bf16[512,1024]{1,0:T(8,128)(2,1)}, u32[]{:S(2)}, u32[]{:S(2)}) collective-permute-start(bf16[512,1024]{1,0:T(8,128)(2,1)S(1)} %pad_maximum_fusion.2.refs_0_), channel_id=1, source_target_pairs={{0,2},{1,3},{2,0},{3,1},{4,6},{5,7},{6,4},{7,5},{8,10},{9,11},{10,... | collective-permute-start | bytes 3145736 | tf_op jit(solution)/shard_map/ppermute | solution.py:347
  48.4 25.1 %collective-permute-start.14 = (bf16[256,1024]{1,0:T(8,128)(2,1)S(1)}, bf16[256,1024]{1,0:T(8,128)(2,1)S(1)}, u32[]{:S(2)}, u32[]{:S(2)}) collective-permute-start(bf16[256,1024]{1,0:T(8,128)(2,1)S(1)} %get-tuple-element.101), channel_id=1, source_target_pairs={{0,16},{1,17},{2,18},{3,19},{4,20},{5,21},{6,22},{7,23},{8,24},{9,... | collective-permute-start | bytes 1572872 | tf_op jit(solution)/shard_map/ppermute | solution.py:347
  50.9 47.0 %collective-permute-start.10 = (bf16[1024,512]{1,0:T(8,128)(2,1)S(1)}, bf16[1024,512]{1,0:T(8,128)(2,1)S(1)}, u32[]{:S(2)}, u32[]{:S(2)}) collective-permute-start(bf16[1024,512]{1,0:T(8,128)(2,1)S(1)} %get-tuple-element.90), channel_id=1, source_target_pairs={{0,8},{1,9},{2,10},{3,11},{4,12},{5,13},{6,14},{7,15},{8,0},{9,1},... | collective-permute-start | bytes 3145736 | tf_op jit(solution)/shard_map/ppermute | solution.py:347
  73.5 23.8 %collective-permute-start.15 = (bf16[256,1024]{1,0:T(8,128)(2,1)S(1)}, bf16[256,1024]{1,0:T(8,128)(2,1)S(1)}, u32[]{:S(2)}, u32[]{:S(2)}) collective-permute-start(bf16[256,1024]{1,0:T(8,128)(2,1)S(1)} %collective-permute-done.14), channel_id=1, source_target_pairs={{0,8},{1,9},{2,10},{3,11},{4,12},{5,13},{6,14},{7,15},{8,0},{9,1},... | collective-permute-start | bytes 1572872 | tf_op jit(solution)/shard_map/ppermute | solution.py:347
  73.5 27.6 %collective-permute-start.7 = (bf16[512,1024]{1,0:T(8,128)(2,1)S(1)}, bf16[512,1024]{1,0:T(8,128)(2,1)}, u32[]{:S(2)}, u32[]{:S(2)}) collective-permute-start(bf16[512,1024]{1,0:T(8,128)(2,1)S(1)} %pad_maximum_fusion.2.refs_0_), channel_id=1, source_target_pairs={{0,1},{1,0},{2,3},{3,2},{4,5},{5,4},{6,7},{7,6},{8,9},{9,8},{10,11... | collective-permute-start | bytes 3145736 | tf_op jit(solution)/shard_map/ppermute | solution.py:347
  73.5 27.6 %collective-permute-start.9 = (bf16[512,1024]{1,0:T(8,128)(2,1)}, bf16[512,1024]{1,0:T(8,128)(2,1)}, u32[]{:S(2)}, u32[]{:S(2)}) collective-permute-start(bf16[512,1024]{1,0:T(8,128)(2,1)} %collective-permute-done.8.refs_2_), channel_id=1, source_target_pairs={{0,1},{1,0},{2,3},{3,2},{4,5},{5,4},{6,7},{7,6},{8,9},{9,8},{10,11... | collective-permute-start | bytes 3145736 | tf_op jit(solution)/shard_map/ppermute | solution.py:347
  97.3 23.1 %collective-permute-start.17 = (bf16[512,1024]{1,0:T(8,128)(2,1)S(1)}, bf16[512,1024]{1,0:T(8,128)(2,1)S(1)}, u32[]{:S(2)}, u32[]{:S(2)}) collective-permute-start(bf16[512,1024]{1,0:T(8,128)(2,1)S(1)} %constant_dynamic-update-slice_fusion.refs_0_), channel_id=1, source_target_pairs={{0,2},{1,3},{2,0},{3,1},{4,6},{5,7},{6,4},{7,5},{8,10},{9,11},{10,... | collective-permute-start | bytes 3145736 | tf_op jit(solution)/shard_map/ppermute | solution.py:347
  98.9 23.1 %collective-permute-start.12 = (bf16[1024,512]{1,0:T(8,128)(2,1)}, bf16[1024,512]{1,0:T(8,128)(2,1)}, u32[]{:S(2)}, u32[]{:S(2)}) collective-permute-start(bf16[1024,512]{1,0:T(8,128)(2,1)} %get-tuple-element.95), channel_id=1, source_target_pairs={{0,8},{1,9},{2,10},{3,11},{4,12},{5,13},{6,14},{7,15},{8,0},{9,1},... | collective-permute-start | bytes 3145736 | tf_op jit(solution)/shard_map/ppermute | solution.py:347
  101.0 31.9 %collective-permute-start.16 = (bf16[512,1024]{1,0:T(8,128)(2,1)S(1)}, bf16[512,1024]{1,0:T(8,128)(2,1)S(1)}, u32[]{:S(2)}, u32[]{:S(2)}) collective-permute-start(bf16[512,1024]{1,0:T(8,128)(2,1)S(1)} %constant_dynamic-update-slice_fusion.refs_0_), channel_id=1, source_target_pairs={{0,1},{1,0},{2,3},{3,2},{4,5},{5,4},{6,7},{7,6},{8,9},{9,8},{10,11... | collective-permute-start | bytes 3145736 | tf_op jit(solution)/shard_map/ppermute | solution.py:347
  111.6 19.9 %collective-permute-start.13 = (bf16[1024,256]{1,0:T(8,128)(2,1)S(1)}, bf16[1024,256]{1,0:T(8,128)(2,1)S(1)}, u32[]{:S(2)}, u32[]{:S(2)}) collective-permute-start(bf16[1024,256]{1,0:T(8,128)(2,1)S(1)} %get-tuple-element.91), channel_id=1, source_target_pairs={{0,4},{1,5},{2,6},{3,7},{4,0},{5,1},{6,2},{7,3},{8,12},{9,13},{10,... | collective-permute-start | bytes 1572872 | tf_op jit(solution)/shard_map/ppermute | solution.py:347
  132.4 19.9 %collective-permute-start.20 = (bf16[1024,128]{1,0:T(8,128)(2,1)}, bf16[1024,128]{1,0:T(8,128)(2,1)}, u32[]{:S(2)}, u32[]{:S(2)}) collective-permute-start(bf16[1024,128]{1,0:T(8,128)(2,1)} %slice.206), channel_id=1, source_target_pairs={{0,16},{1,17},{2,18},{3,19},{4,20},{5,21},{6,22},{7,23},{8,24},{9,... | collective-permute-start | bytes 786440 | tf_op jit(solution)/shard_map/ppermute | solution.py:347
  137.6 21.5 %collective-permute-start.21 = (bf16[1024,256]{1,0:T(8,128)(2,1)}, bf16[1024,256]{1,0:T(8,128)(2,1)}, u32[]{:S(2)}, u32[]{:S(2)}) collective-permute-start(bf16[1024,256]{1,0:T(8,128)(2,1)} %get-tuple-element.112), channel_id=1, source_target_pairs={{0,4},{1,5},{2,6},{3,7},{4,0},{5,1},{6,2},{7,3},{8,12},{9,13},{10,... | collective-permute-start | bytes 1572872 | tf_op jit(solution)/shard_map/ppermute | solution.py:347
  151.5 58.2 %collective-permute-start.29 = (bf16[512,1024]{1,0:T(8,128)(2,1)}, bf16[512,1024]{1,0:T(8,128)(2,1)S(1)}, u32[]{:S(2)}, u32[]{:S(2)}) collective-permute-start(bf16[512,1024]{1,0:T(8,128)(2,1)} %copy-done.32), channel_id=1, source_target_pairs={{0,8},{1,9},{2,10},{3,11},{4,12},{5,13},{6,14},{7,15},{8,0},{9,1},... | collective-permute-start | bytes 3145736 | tf_op jit(solution)/shard_map/ppermute | solution.py:347
  152.3 29.5 %collective-permute-start.28 = (bf16[1024,128]{1,0:T(8,128)(2,1)}, bf16[1024,128]{1,0:T(8,128)(2,1)S(1)}, u32[]{:S(2)}, u32[]{:S(2)}) collective-permute-start(bf16[1024,128]{1,0:T(8,128)(2,1)} %slice.207), channel_id=1, source_target_pairs={{0,16},{1,17},{2,18},{3,19},{4,20},{5,21},{6,22},{7,23},{8,24},{9,... | collective-permute-start | bytes 786440 | tf_op jit(solution)/shard_map/ppermute | solution.py:347
  160.6 29.5 %collective-permute-start.22 = (bf16[1024,128]{1,0:T(8,128)(2,1)S(1)}, bf16[1024,128]{1,0:T(8,128)(2,1)S(1)}, u32[]{:S(2)}, u32[]{:S(2)}) collective-permute-start(bf16[1024,128]{1,0:T(8,128)(2,1)S(1)} %slice.204), channel_id=1, source_target_pairs={{0,16},{1,17},{2,18},{3,19},{4,20},{5,21},{6,22},{7,23},{8,24},{9,... | collective-permute-start | bytes 786440 | tf_op jit(solution)/shard_map/ppermute | solution.py:347
  164.9 25.5 %collective-permute-start.23 = (bf16[1024,256]{1,0:T(8,128)(2,1)S(1)}, bf16[1024,256]{1,0:T(8,128)(2,1)S(1)}, u32[]{:S(2)}, u32[]{:S(2)}) collective-permute-start(bf16[1024,256]{1,0:T(8,128)(2,1)S(1)} %get-tuple-element.117), channel_id=1, source_target_pairs={{0,4},{1,5},{2,6},{3,7},{4,0},{5,1},{6,2},{7,3},{8,12},{9,13},{10,... | collective-permute-start | bytes 1572872 | tf_op jit(solution)/shard_map/ppermute | solution.py:347
  167.7 22.4 %collective-permute-start.27 = (bf16[1024,128]{1,0:T(8,128)(2,1)S(1)}, bf16[1024,128]{1,0:T(8,128)(2,1)S(1)}, u32[]{:S(2)}, u32[]{:S(2)}) collective-permute-start(bf16[1024,128]{1,0:T(8,128)(2,1)S(1)} %slice.202), channel_id=1, source_target_pairs={{0,16},{1,17},{2,18},{3,19},{4,20},{5,21},{6,22},{7,23},{8,24},{9,... | collective-permute-start | bytes 786440 | tf_op jit(solution)/shard_map/ppermute | solution.py:347
  256.9 24.2 %collective-permute-start.44 = (bf16[512,512]{1,0:T(8,128)(2,1)}, bf16[512,512]{1,0:T(8,128)(2,1)}, u32[]{:S(2)}, u32[]{:S(2)}) collective-permute-start(bf16[512,512]{1,0:T(8,128)(2,1)} %copy-done.33), channel_id=1, source_target_pairs={{0,4},{1,5},{2,6},{3,7},{4,0},{5,1},{6,2},{7,3},{8,12},{9,13},{10,... | collective-permute-start | bytes 1572872 | tf_op jit(solution)/shard_map/ppermute | solution.py:347
  258.4 24.2 %collective-permute-start.42 = (bf16[2,2,8,64,128]{4,3,2,1,0:T(8,128)(2,1)S(1)}, bf16[2,2,8,64,128]{4,3,2,1,0:T(8,128)(2,1)S(1)}, u32[]{:S(2)}, u32[]{:S(2)}) collective-permute-start(bf16[2,2,8,64,128]{4,3,2,1,0:T(8,128)(2,1)S(1)} %pad_maximum_fusion.11.own_0), channel_id=1, source_target_pairs={{0,1},{1,0},{2,3},{3,2},{4,5},{5,4},{6,7},{7,6},{8,9},{9,8},{10,11... | collective-permute-start | bytes 1572872 | tf_op jit(solution)/shard_map/ppermute | solution.py:347
  262.2 20.4 %collective-permute-start.43 = (bf16[2,2,8,64,128]{4,3,2,1,0:T(8,128)(2,1)}, bf16[2,2,8,64,128]{4,3,2,1,0:T(8,128)(2,1)S(1)}, u32[]{:S(2)}, u32[]{:S(2)}) collective-permute-start(bf16[2,2,8,64,128]{4,3,2,1,0:T(8,128)(2,1)} %collective-permute-done.41.own_1), channel_id=1, source_target_pairs={{0,1},{1,0},{2,3},{3,2},{4,5},{5,4},{6,7},{7,6},{8,9},{9,8},{10,11... | collective-permute-start | bytes 1572872 | tf_op jit(solution)/shard_map/ppermute | solution.py:347
  272.9 21.4 %collective-permute-start.46 = (bf16[256,512]{1,0:T(8,128)(2,1)S(1)}, bf16[256,512]{1,0:T(8,128)(2,1)S(1)}, u32[]{:S(2)}, u32[]{:S(2)}) collective-permute-start(bf16[256,512]{1,0:T(8,128)(2,1)S(1)} %slice.200), channel_id=1, source_target_pairs={{0,16},{1,17},{2,18},{3,19},{4,20},{5,21},{6,22},{7,23},{8,24},{9,... | collective-permute-start | bytes 786440 | tf_op jit(solution)/shard_map/ppermute | solution.py:347
  299.2 27.8 %collective-permute-start.50 = (bf16[128,1024]{1,0:T(8,128)(2,1)S(1)}, bf16[128,1024]{1,0:T(8,128)(2,1)S(1)}, u32[]{:S(2)}, u32[]{:S(2)}) collective-permute-start(bf16[128,1024]{1,0:T(8,128)(2,1)S(1)} %pad_maximum_fusion.15), channel_id=1, source_target_pairs={{0,8},{1,9},{2,10},{3,11},{4,12},{5,13},{6,14},{7,15},{8,0},{9,1},... | collective-permute-start | bytes 786440 | tf_op jit(solution)/shard_map/ppermute | solution.py:347
  301.5 19.1 %collective-permute-start.52 = (bf16[256,512]{1,0:T(8,128)(2,1)S(1)}, bf16[256,512]{1,0:T(8,128)(2,1)S(1)}, u32[]{:S(2)}, u32[]{:S(2)}) collective-permute-start(bf16[256,512]{1,0:T(8,128)(2,1)S(1)} %slice.198), channel_id=1, source_target_pairs={{0,16},{1,17},{2,18},{3,19},{4,20},{5,21},{6,22},{7,23},{8,24},{9,... | collective-permute-start | bytes 786440 | tf_op jit(solution)/shard_map/ppermute | solution.py:347
  (75 other events, 685.4 us)
